TPU v7x, 512 devices: a whole 4x4x16 slice. The times are simulated.
512 devices in a mesh: geo: 64 (over z, y), cell: 8 (over x, core).
Axes of the slice: x: 4, y: 4, z: 16, core: 2. Of those that a mesh axis runs over, the one named last changes fastest.
Arguments:
- detail_rows: float32 [8192, 2048], P('geo', 'cell'), may hold values from -60 to 60
- row_block: int32 [8192], P('geo'), may hold values from 0 to 8191, as said below
- block_weight: int32 [8192], P('geo'), may hold values from 1 to 9
- block_group: int32 [8192], P('geo'), may hold values from 0 to 63, as said below
- query_matrix: int32 [2048, 512], P('cell'), may hold values 0 or 1
- query_weight: float32 [512], replicated, may hold values from 0.0048828125 to 0.048828125
- query_noisy: float32 [8192, 512], P('geo'), may hold values from -48 to 48
- group_noisy: float32 [64, 2048], P(None, 'cell'), may hold values from -48 to 48
Outputs:
- solution_field: float32 [8192, 2048], P('geo', 'cell')
- residual: float32 [8192, 2048], P('geo', 'cell')
Inputs may be any that keep to these rules, and one draw needn't show every extreme that they name: row_block is a permutation of all blocks; arrival row r lies on geo index r // 128 and its block lies on geo index (r mod 128) // 2, so each geo index sends 2 rows to each geo index. `block_group`: every group holds exactly 128 blocks.
All inputs are finite; a program needn't handle non-finite values. No bound on the sum of `query_matrix` on one device may be relied on, other than what follows from the above.
Results may differ from a plain program's by a relative error of at most 0.0029.
Values sent between devices are 32-bit elements; how exact they have to be, the bound alone decides.
A program may use at most 64 MiB of HBM per device.

v0:
```python
import jax
import jax.numpy as jnp
from jax import lax
from jax.sharding import PartitionSpec as P

QUERIES = 512
ITERS = 2
BLK_DEV = 128


AGG_WEIGHT = 0.25
HIGHEST_PREC = lax.Precision.HIGHEST
LEADING_DIMS = (((0,), (1,)), ((), ()))


def local(
    detail_rows,
    row_block,
    block_weight,
    block_group,
    query_matrix,
    query_weight,
    query_noisy,
    group_noisy,
):
    geo_index = lax.axis_index("geo")
    sent_ids = row_block.astype(jnp.float32)
    rows_in, ids_in = (
        lax.all_to_all(detail_rows, "geo", split_axis=0, concat_axis=0, tiled=True),
        lax.all_to_all(sent_ids, "geo", split_axis=0, concat_axis=0, tiled=True),
    )
    local_rows = ids_in.astype(jnp.int32) - geo_index * BLK_DEV
    detail = jnp.zeros(detail_rows.shape, jnp.float32).at[local_rows].set(rows_in)
    weight = block_weight.astype(jnp.float32)[:, None]
    queries = query_matrix.astype(jnp.float32)
    group_count = group_noisy.shape[0]
    share_rows = QUERIES // lax.axis_size("cell")

    def squares(vector):
        return lax.psum(jnp.sum(vector * vector), ("geo", "cell"))

    right_side = weight * detail
    right_side = right_side + jnp.dot(
        query_noisy * query_weight[None, :],
        queries.T,
        precision=HIGHEST_PREC,
        preferred_element_type=jnp.float32,
    )
    right_side = right_side + AGG_WEIGHT * group_noisy[block_group]
    solution_field = jnp.zeros_like(right_side)
    residual = right_side
    direction = right_side
    norm_now = squares(residual)
    for iteration in range(ITERS):
        partial_totals = jax.ops.segment_sum(direction, block_group, num_segments=group_count)
        totals = lax.psum(partial_totals, "geo")
        estimate = direction
        share_part = lax.psum_scatter(
            lax.dot_general(
                queries,
                estimate,
                LEADING_DIMS,
                precision=HIGHEST_PREC,
                preferred_element_type=jnp.float32,
            ),
            "cell",
            scatter_dimension=0,
            tiled=True,
        )
        scales = lax.dynamic_slice_in_dim(
            query_weight, lax.axis_index("cell") * share_rows, share_rows, 0
        )
        share_part = share_part * scales[:, None]
        spread_back = lax.dot_general(
            lax.all_gather(share_part, "cell", axis=0, tiled=True),
            queries,
            LEADING_DIMS,
            precision=HIGHEST_PREC,
            preferred_element_type=jnp.float32,
        )
        image_vec = weight * direction + spread_back + AGG_WEIGHT * totals[block_group]
        step_size = norm_now / lax.psum(jnp.sum(direction * image_vec), ("geo", "cell"))
        solution_field = solution_field + step_size * direction
        residual = residual - step_size * image_vec
        norm_next = squares(residual)
        direction = residual + norm_next / norm_now * direction
        norm_now = norm_next
    return (solution_field, residual)


def solution(mesh):
    return jax.shard_map(
        local,
        mesh=mesh,
        in_specs=(
            P("geo", "cell"),
            P("geo"),
            P("geo"),
            P("geo"),
            P("cell", None),
            P(),
            P("geo", None),
            P(None, "cell"),
        ),
        out_specs=(P("geo", "cell"), P("geo", "cell")),
        check_vma=False,
    )
```

profile of v0, /device:TPU:1, one launch (start us, length us, event | category | flops | bytes accessed | tf_op | source)
XLA Modules:
  0.0 915.7 jit_solution(15356650263555236824)
XLA Ops:
  8.0 0.7 convert_element_type.21
  8.7 0.8 all_to_all.14
  9.5 19.3 %all-to-all-start = ((f32[64,2,1]{1,2,0:T(1,128)}), f32[64,2,1]{1,2,0:T(1,128)S(1)}, u32[]{:S(2)}, u32[]{:S(2)}) async-start(f32[64,2,1]{1,2,0:T(1,128)} %bitcast), calls=%async_computation | async-start | bytes 65536 | tf_op jit(solution)/shard_map/all_to_all | solution.py:30
  28.7 1.6 all_to_all.16
  30.4 11.7 %all-to-all-done = f32[64,2,1]{1,2,0:T(1,128)S(1)} async-done(((f32[64,2,1]{1,2,0:T(1,128)}), f32[64,2,1]{1,2,0:T(1,128)S(1)}, u32[]{:S(2)}, u32[]{:S(2)}) %all-to-all-start) | async-done | bytes 544 | tf_op jit(solution)/shard_map/all_to_all | solution.py:30
  42.1 4.6 all-to-all-start.1
  46.8 0.6 copy-done.4
  47.5 0.8 gather_fusion
  48.6 13.3 %all-to-all-done.1 = f32[64,2,256]{2,1,0:T(2,128)S(1)} async-done(((f32[64,2,256]{2,1,0:T(2,128)}), f32[64,2,256]{2,1,0:T(2,128)S(1)}, u32[]{:S(2)}, u32[]{:S(2)}) %all-to-all-start.1) | async-done | bytes 131104 | tf_op jit(solution)/shard_map/all_to_all | solution.py:29
  62.0 1.0 scatter_custom_fusion
  63.1 0.7 fusion.2
  63.8 1.8 scatter_custom_fusion.1
  65.7 0.4 convolution_bitcast_fusion.1
  66.1 0.8 copy.16
  67.1 238.7 %all-reduce.4.cloned.1.call-done = f32[64,256]{1,0:T(8,128)} async-done(((f32[64,256]{1,0:T(8,128)}), f32[64,256]{1,0:T(8,128)}) %all-reduce.4.cloned.1.call-update) | async-done | bytes 65552 | tf_op jit(solution)/shard_map/psum | solution.py:56
  305.8 1.6 gather_fusion.1
  307.4 0.8 broadcast_multiply_fusion.1
  308.3 23.9 %all_gather.6 = f32[512,128]{1,0:T(8,128)S(1)} all-gather(f32[64,128]{1,0:T(8,128)S(1)} %broadcast_multiply_fusion.1), channel_id=1, replica_groups=mesh['geo'=64,'cell'=8] {'cell'}, dimensions={0}, use_global_device_ids=true | all-gather | bytes 294912 | tf_op jit(solution)/shard_map/all_gather | solution.py:75
  332.2 1.2 multiply_reduce_fusion.2
  333.4 100.5 %all-reduce = (f32[]{:T(128)}, f32[]{:T(128)}) all-reduce(f32[]{:T(128)} %get-tuple-element.3, f32[]{:T(128)} %get-tuple-element.2), channel_id=1, replica_groups=mesh['geo'=64,'cell'=8] {'geo','cell'}, use_global_device_ids=true, to_apply=%region_2.0 | all-reduce | flops 2 | bytes 16 | tf_op jit(solution)/shard_map/psum | solution.py:40
  435.2 0.6 multiply_reduce_fusion.1
  435.8 99.4 %psum.45 = f32[]{:T(128)} all-reduce(f32[]{:T(128)} %multiply_reduce_fusion.1), channel_id=1, replica_groups=mesh['geo'=64,'cell'=8] {'geo','cell'}, use_global_device_ids=true, to_apply=%region_9.0 | all-reduce | flops 1 | bytes 8 | tf_op jit(solution)/shard_map/psum | solution.py:40
  536.6 1.8 scatter_custom_fusion.2
  538.5 0.4 convolution_bitcast_fusion
  538.9 0.8 copy.18
  539.8 238.5 %all-reduce.6.cloned.1.call-done = f32[64,256]{1,0:T(8,128)} async-done(((f32[64,256]{1,0:T(8,128)}), f32[64,256]{1,0:T(8,128)}) %all-reduce.6.cloned.1.call-update) | async-done | bytes 65552 | tf_op jit(solution)/shard_map/psum | solution.py:56
  778.3 1.6 gather_fusion.2
  779.9 0.8 broadcast_multiply_fusion
  780.7 23.9 %all_gather.7 = f32[512,128]{1,0:T(8,128)S(1)} all-gather(f32[64,128]{1,0:T(8,128)S(1)} %broadcast_multiply_fusion), channel_id=1, replica_groups=mesh['geo'=64,'cell'=8] {'cell'}, dimensions={0}, use_global_device_ids=true | all-gather | bytes 294912 | tf_op jit(solution)/shard_map/all_gather | solution.py:75
  804.6 1.2 multiply_reduce_fusion
  805.8 100.4 %psum.47 = f32[]{:T(128)} all-reduce(f32[]{:T(128)} %get-tuple-element.9), channel_id=1, replica_groups=mesh['geo'=64,'cell'=8] {'geo','cell'}, use_global_device_ids=true, to_apply=%region_14.0 | all-reduce | flops 1 | bytes 8 | tf_op jit(solution)/shard_map/psum | solution.py:82
  907.5 0.7 multiply_subtract_fusion
  (30 shorter events, 0.8 us)
Async XLA Ops:
  8.0 39.5 %copy-start = (f32[64,256]{1,0:T(8,128)S(1)}, f32[64,256]{1,0:T(8,128)}, u32[]{:S(2)}) copy-start(f32[64,256]{1,0:T(8,128)} %param.15) | copy-start | bytes 196612
  9.5 32.7 %all-to-all-start = ((f32[64,2,1]{1,2,0:T(1,128)}), f32[64,2,1]{1,2,0:T(1,128)S(1)}, u32[]{:S(2)}, u32[]{:S(2)}) async-start(f32[64,2,1]{1,2,0:T(1,128)} %bitcast), calls=%async_computation | async-start | bytes 65536 | tf_op jit(solution)/shard_map/all_to_all | solution.py:30
  30.4 16.4 %copy-start.5 = (s32[128]{0:T(128)S(1)}, s32[128]{0:T(128)}, u32[]{:S(2)}) copy-start(s32[128]{0:T(128)} %param.11) | copy-start | bytes 1540
  42.1 19.8 %all-to-all-start.1 = ((f32[64,2,256]{2,1,0:T(2,128)}), f32[64,2,256]{2,1,0:T(2,128)S(1)}, u32[]{:S(2)}, u32[]{:S(2)}) async-start(f32[64,2,256]{2,1,0:T(2,128)} %all_to_all.16), calls=%async_computation.1 | async-start | bytes 262144 | tf_op jit(solution)/shard_map/all_to_all | solution.py:29
  46.8 259.0 %all-reduce.4.cloned.1.call-start = ((), (), s32[]{:S(2)}) async-start(), calls=%async_computation.4 | async-start | bytes 131072 | tf_op jit(solution)/shard_map/psum | solution.py:56
  46.8 0.7 copy-start.4
  47.5 15.6 %copy-start.1 = (s32[256,512]{1,0:T(8,128)S(1)}, s32[256,512]{1,0:T(8,128)}, u32[]{:S(2)}) copy-start(s32[256,512]{1,0:T(8,128)} %param.12) | copy-start | bytes 1572868
  48.3 14.8 %copy-start.2 = (f32[128,512]{1,0:T(8,128)S(1)}, f32[128,512]{1,0:T(8,128)}, u32[]{:S(2)}) copy-start(f32[128,512]{1,0:T(8,128)} %param.14) | copy-start | bytes 786436
  62.0 1.1 copy-start.3
  65.6 241.8 %reduce-scatter.7.cloned.1.call-start = ((), (), s32[]{:S(2)}) async-start(), calls=%async_computation.6 | async-start | bytes 294912 | tf_op jit(solution)/shard_map/reduce_scatter | solution.py:58
  67.0 711.3 %all-reduce.6.cloned.1.call-start = ((), (), s32[]{:S(2)}) async-start(), calls=%async_computation.5 | async-start | bytes 131072 | tf_op jit(solution)/shard_map/psum | solution.py:56
  538.4 241.5 %reduce-scatter.9.cloned.1.call-start = ((), (), s32[]{:S(2)}) async-start(), calls=%async_computation.7 | async-start | bytes 294912 | tf_op jit(solution)/shard_map/reduce_scatter | solution.py:58
Sparse Core Ops, SparseCore 0:
  65.8 239.9 all-reduce.3
  538.5 239.6 all-reduce.5
Sparse Core Ops, SparseCore 1:
  68.9 29.8 reduce-scatter.6
  541.9 28.9 reduce-scatter.8
where the time goes:
time: 917 us; the launch traced here: 916 us
  waiting for transfers between devices  502 us (55%)
  blocking collectives  348 us (38%)
  starting transfers between devices  24.1 us (3%)
  between operations  19.7 us (2%)
  local copies, waits for them, and re-layouts  10 us (1%)
    psum x2, waiting for transfers between devices, local(): totals = lax.psum(partial_totals, 'geo')  477 us
    psum x2, blocking collectives, squares(): return lax.psum(jnp.sum(vector * vector), ('geo', 'cell'))  200 us
    psum x1, blocking collectives, local(): lax.psum(jnp.sum(direction * image_vec), ('geo', 'cell'))  100 us
    all_gather x2, blocking collectives, local(): lax.all_gather(share_part, 'cell', axis=0, tiled=True)  47.8 us
    all_to_all x1, starting transfers between devices, local(): lax.all_to_all(sent_ids, 'geo', split_axis=0, concat_axis=0, tiled=True)  19.3 us
  transfers between devices with their start and end apart: 6, of which 4 were waited for; matrix products, arithmetic and copies ran while one was open for 1% of the time, Pallas kernels for 0%

commit v1 on v0

v1 whole, which is shorter than its diff:
```python
import functools
import jax
import jax.numpy as jnp
from jax import lax
from jax.experimental import pallas as pl
from jax.experimental.pallas import tpu as pltpu
from jax.sharding import PartitionSpec as P

NZ, NY, NX, NC = 16, 4, 4, 2
GROUP_SIZE = 128.0
F32, BF16 = jnp.float32, jnp.bfloat16
NN = (((1,), (0,)), ((), ()))
NT = (((1,), (1,)), ((), ()))
TN = (((0,), (0,)), ((), ()))


def parts(x, n):
    out = []
    for i in range(n):
        p = x.astype(BF16)
        out.append(p)
        if i < n - 1:
            x = x - p.astype(F32)
    return out


def mxu(a, b, dims):
    return lax.dot_general(a, b, dims, preferred_element_type=F32)


def dot_l(x, y, dims, n=3):
    return functools.reduce(lambda s, p: s + p, [mxu(p, y, dims) for p in parts(x, n)])


def dot_r(x, y, dims, n=3):
    return functools.reduce(lambda s, p: s + p, [mxu(x, p, dims) for p in parts(y, n)])


def fold(v):
    s = jnp.sum(v, axis=0, keepdims=True)
    return functools.reduce(
        lambda p, q: p + q, [s[:, i : i + 128] for i in range(0, s.shape[1], 128)]
    )


def spread_order(n):
    return sorted(range(1, n), key=lambda k: -min(k, n - k))


def scratch_of(blk, cells, queries, groups):
    share = blk // (NX * NC)
    half = queries // NC
    zr = blk // NZ
    dma = pltpu.SemaphoreType.DMA
    return {
        "qi": pltpu.VMEM((cells, queries), jnp.int32),
        "qb": pltpu.VMEM((cells, queries), BF16),
        "rbv": pltpu.VMEM((1, blk), jnp.int32),
        "bwv": pltpu.VMEM((1, blk), jnp.int32),
        "bgv": pltpu.VMEM((1, blk), jnp.int32),
        "qwv": pltpu.VMEM((1, queries), F32),
        "qnv": pltpu.VMEM((blk, queries), F32),
        "gnv": pltpu.VMEM((groups, cells), F32),
        "ar": pltpu.VMEM((NZ, zr, cells), F32),
        "ai": pltpu.VMEM((NZ, 1, blk), jnp.int32),
        "sy": pltpu.VMEM((NY, zr // NY, NZ, cells), F32),
        "br": pltpu.VMEM((NY, zr // NY, NZ, cells), F32),
        "bi": pltpu.VMEM((NY, NZ, 1, blk), jnp.int32),
        "tp": pltpu.VMEM((groups, 3 * cells + 128), F32),
        "ty": pltpu.VMEM((NY, NZ, 3 * cells + 128), F32),
        "pz": pltpu.VMEM((NZ, 8, 128), F32),
        "tz": pltpu.VMEM((NZ, 8, 128), F32),
        "ex": pltpu.VMEM((16, 128), F32),
        "exr": pltpu.VMEM((NX * NC, 16, 128), F32),
        "mp": pltpu.VMEM((blk, queries), F32),
        "mr": pltpu.VMEM((NX * NC, share, queries), F32),
        "ms": pltpu.VMEM((share, queries), F32),
        "mf": pltpu.VMEM((blk, queries), F32),
        "gp": pltpu.VMEM((queries, queries), F32),
        "gc": pltpu.VMEM((half, queries), F32),
        "gh": pltpu.VMEM((half, queries), F32),
        "gr": pltpu.VMEM((NX, half // NX, queries), F32),
        "gf": pltpu.VMEM((queries, queries), F32),
        "az": pltpu.VMEM((8, 128), F32),
        "azr": pltpu.VMEM((NZ, 8, 128), F32),
        "ay": pltpu.VMEM((NZ, 640), F32),
        "ayr": pltpu.VMEM((NY, NZ, 640), F32),
        "base": pltpu.VMEM((blk, cells), F32),
        "bv": pltpu.VMEM((blk, cells), F32),
        "load": dma((10,)),
        "z_s": dma((NZ,)), "z_r": dma((NZ,)), "zi_s": dma((NZ,)), "zi_r": dma((NZ,)),
        "y_s": dma((NY,)), "y_r": dma((NY,)), "yi_s": dma((NY,)), "yi_r": dma((NY,)),
        "ty_s": dma((NY,)), "ty_r": dma((NY,)),
        "tz_s": dma((NZ,)), "tz_r": dma((NZ,)),
        "ex_s": dma((NX * NC,)), "ex_r": dma((NX * NC,)),
        "mr_s": dma((NX * NC,)), "mr_r": dma((NX * NC,)),
        "ma_s": dma((NX * NC,)), "ma_r": dma((NX * NC,)),
        "gc_s": dma((2,)), "gc_r": dma((2,)),
        "gr_s": dma((NX,)), "gr_r": dma((NX,)),
        "ga_s": dma((NX,)), "ga_r": dma((NX,)),
        "az_s": dma((NZ,)), "az_r": dma((NZ,)),
        "ay_s": dma((NY,)), "ay_r": dma((NY,)),
    }


def kernel(names, dr, rb, bw, bg, qm, qw, qn, gn, x_out, r_out, *refs):
    s = dict(zip(names, refs))
    blk, cells = dr.shape
    queries = qm.shape[1]
    groups = gn.shape[0]
    n_cell = NX * NC
    zr = blk // NZ
    sr = zr // NY
    share = blk // n_cell
    half = queries // NC
    hx = half // NX
    geo = lax.axis_index("geo")
    cell = lax.axis_index("cell")
    z, y = geo // NY, lax.rem(geo, NY)
    x, core = cell // NC, lax.rem(cell, NC)
    mate = 1 - core
    sends = []

    def to_z(k):
        return lax.rem(z + k, NZ)

    def to_y(k):
        return lax.rem(y + k, NY)

    def to_x(k):
        return lax.rem(x + k, NX)

    def to_c(k):
        return lax.rem(cell + k, n_cell)

    def z_peer(k):
        return (to_z(k) * NY + y, cell)

    def y_peer(k):
        return (z * NY + to_y(k), cell)

    def x_peer(k):
        return (geo, to_x(k) * NC + core)

    def c_peer(k):
        return (geo, to_c(k))

    mate_peer = (geo, x * NC + mate)

    def remote(src, dst, name, k, peer):
        return pltpu.make_async_remote_copy(
            src_ref=src,
            dst_ref=dst,
            send_sem=s[name + "_s"].at[k],
            recv_sem=s[name + "_r"].at[k],
            device_id=peer,
            device_id_type=pl.DeviceIdType.MESH,
        )

    def send(*a):
        copy = remote(*a)
        copy.start()
        sends.append(copy)

    def arrived(dst, name, k, peer):
        remote(dst, dst, name, k, peer).wait_recv()

    loads = [
        pltpu.make_async_copy(src, dst, s["load"].at[i])
        for i, (src, dst) in enumerate(
            [
                (qm, s["qi"]),
                (bw, s["bwv"]),
                (bg, s["bgv"]),
                (qw, s["qwv"]),
                (qn, s["qnv"]),
                (gn, s["gnv"]),
                (dr.at[pl.ds(pl.multiple_of(z * zr, zr), zr)], s["ar"].at[z]),
                (rb, s["ai"].at[z]),
            ]
        )
    ]
    for copy in loads:
        copy.start()

    barrier = pltpu.get_barrier_semaphore()
    greet = (
        [z_peer(k) for k in range(1, NZ)]
        + [y_peer(k) for k in range(1, NY)]
        + [c_peer(k) for k in range(1, n_cell)]
    )
    for peer in greet:
        pl.semaphore_signal(barrier, inc=1, device_id=peer, device_id_type=pl.DeviceIdType.MESH)

    loads[0].wait()
    s["qb"][...] = s["qi"][...].astype(F32).astype(BF16)
    qb = s["qb"]
    s["gp"][...] = mxu(qb[...], qb[...], TN)
    pl.semaphore_wait(barrier, len(greet))

    for k in spread_order(NZ):
        row0 = pl.multiple_of(to_z(k) * zr, zr)
        send(dr.at[pl.ds(row0, zr)], s["ar"].at[z], "z", k, z_peer(k))
        send(rb, s["ai"].at[z], "zi", k, z_peer(k))
    send(s["gp"].at[pl.ds(pl.multiple_of(mate * half, half), half)], s["gc"], "gc", 0, mate_peer)

    for copy in loads[1:]:
        copy.wait()
    eye = lax.broadcasted_iota(jnp.int32, (blk, blk), 0) == lax.broadcasted_iota(jnp.int32, (blk, blk), 1)
    w = jnp.sum(jnp.where(eye, s["bwv"][...].astype(F32), 0.0), axis=1, keepdims=True)
    bg_col = jnp.sum(jnp.where(eye, s["bgv"][...].astype(F32), 0.0), axis=1, keepdims=True)
    pick = (bg_col == lax.broadcasted_iota(jnp.int32, (blk, groups), 1).astype(F32)).astype(F32).astype(BF16)
    gather = (s["bgv"][...] == lax.broadcasted_iota(jnp.int32, (groups, blk), 0)).astype(F32).astype(BF16)
    qw_row = s["qwv"][...]
    s["base"][...] = dot_l(s["qnv"][...] * qw_row, qb[...], NT) + 0.25 * dot_r(pick, s["gnv"][...], NN)

    arrived(s["gc"], "gc", 0, mate_peer)
    s["gh"][...] = s["gp"][pl.ds(pl.multiple_of(core * half, half), half)] + s["gc"][...]
    for k in spread_order(NX):
        send(s["gh"].at[pl.ds(pl.multiple_of(to_x(k) * hx, hx), hx)], s["gr"].at[k], "gr", k, x_peer(k))

    for k in spread_order(NZ)[::-1]:
        src = to_z(NZ - k)
        arrived(s["ar"].at[src], "z", k, z_peer(k))
        arrived(s["ai"].at[src], "zi", k, z_peer(k))
    for yy in range(NY):
        for kk in range(sr):
            s["sy"][yy, kk] = s["ar"][:, yy * sr + kk, :]
    for k in spread_order(NY):
        send(s["sy"].at[to_y(k)], s["br"].at[y], "y", k, y_peer(k))
        send(s["ai"], s["bi"].at[y], "yi", k, y_peer(k))
    s["br"][y] = s["sy"][y]
    s["bi"][y] = s["ai"][...]

    for k in range(1, NX):
        arrived(s["gr"].at[k], "gr", k, x_peer(k))
    mine = pl.ds(pl.multiple_of(core * half + x * hx, hx), hx)
    total = s["gh"][pl.ds(pl.multiple_of(x * hx, hx), hx)]
    for k in range(1, NX):
        total = total + s["gr"][k]
    s["gf"][mine] = total
    for k in spread_order(NX):
        send(s["gf"].at[mine], s["gf"].at[mine], "ga", k, x_peer(k))

    for k in spread_order(NY)[::-1]:
        src = to_y(NY - k)
        arrived(s["br"].at[src], "y", k, y_peer(k))
        arrived(s["bi"].at[src], "yi", k, y_peer(k))

    ids = s["bi"][...].reshape(NY * NZ, blk).astype(F32)
    lane = lax.broadcasted_iota(jnp.int32, (NY * NZ, blk), 1)
    id_col = jnp.concatenate(
        [
            jnp.sum(jnp.where(lane == geo * sr + kk, ids, 0.0), axis=1, keepdims=True)
            for kk in range(sr)
        ],
        axis=0,
    )
    rows = jnp.concatenate([s["br"][:, kk].reshape(NY * NZ, cells) for kk in range(sr)], axis=0)
    here = lax.broadcasted_iota(jnp.int32, (blk, blk), 1) + geo * blk
    place = (id_col == here.astype(F32)).astype(F32).astype(BF16)
    detail = dot_r(place, rows, TN)

    b = w * detail + s["base"][...]
    s["bv"][...] = b
    wb = w * b
    wwb = w * wb
    s["tp"][...] = dot_r(
        gather, jnp.concatenate([b, wb, wwb, jnp.broadcast_to(w, (blk, 128))], axis=1), NN
    )
    for k in spread_order(NY):
        send(s["tp"].at[pl.ds(pl.multiple_of(to_y(k) * NZ, NZ), NZ)], s["ty"].at[k], "ty", k, y_peer(k))
    s["mp"][...] = dot_l(b, qb[...], NN)
    for k in range(1, n_cell):
        send(s["mp"].at[pl.ds(pl.multiple_of(to_c(k) * share, share), share)], s["mr"].at[k], "mr", k, c_peer(k))
    scal_b = [fold(b * b), fold(b * wb), fold(wb * wb), fold(wb * wwb)]

    for k in range(1, NY):
        arrived(s["ty"].at[k], "ty", k, y_peer(k))
    t = s["tp"][pl.ds(pl.multiple_of(y * NZ, NZ), NZ)]
    for k in range(1, NY):
        t = t + s["ty"][k]
    for i, row in enumerate([0, 4, 1, 5, 2, 6, 3]):
        s["pz"][:, row, :] = t[:, i * 128 : (i + 1) * 128]
    s["pz"][:, 7, :] = jnp.zeros((NZ, 128), F32)
    for k in spread_order(NZ):
        send(s["pz"].at[to_z(k)], s["tz"].at[k], "tz", k, z_peer(k))

    for k in range(1, n_cell):
        arrived(s["mr"].at[k], "mr", k, c_peer(k))
    own = pl.ds(pl.multiple_of(cell * share, share), share)
    m_own = s["mp"][own]
    for k in range(1, n_cell):
        m_own = m_own + s["mr"][k]
    s["mf"][own] = m_own
    for k in range(1, n_cell):
        send(s["mf"].at[own], s["mf"].at[own], "ma", k, c_peer(k))

    for k in spread_order(NZ)[::-1]:
        arrived(s["tz"].at[k], "tz", k, z_peer(k))
    t = s["pz"][z]
    for k in range(1, NZ):
        t = t + s["tz"][k]
    q0 = dot_l(t, qb[:128], NN)
    q1 = dot_l(t, qb[128:], NN)
    tq = q0[0:2] + q1[4:6]
    t0, t1, t2 = [jnp.concatenate([t[i : i + 1], t[i + 4 : i + 5]], axis=0) for i in range(3)]
    s["ex"][...] = jnp.concatenate(
        [tq[i : i + 1, j : j + 128] for i in range(2) for j in range(0, queries, 128)]
        + scal_b
        + [fold(t0 * t0), fold(t0 * t1), fold(t0 * t2), fold(t1 * t1)],
        axis=0,
    )
    for k in range(1, n_cell):
        send(s["ex"], s["exr"].at[k], "ex", k, c_peer(k))

    for k in range(1, NX):
        src = pl.ds(pl.multiple_of(core * half + to_x(NX - k) * hx, hx), hx)
        arrived(s["gf"].at[src], "ga", k, x_peer(k))
    held = s["gf"].at[pl.ds(pl.multiple_of(core * half, half), half)]
    send(held, held, "gc", 1, mate_peer)

    for k in range(1, n_cell):
        src = pl.ds(pl.multiple_of(to_c(n_cell - k) * share, share), share)
        arrived(s["mf"].at[src], "ma", k, c_peer(k))
    m = s["mf"][...]
    f = m * qw_row
    b = s["bv"][...]
    u = w * b + dot_l(f, qb[...], NT)
    fm = f * m
    sum_fm, sum_wfm, sum_wwfm = fold(fm), fold(w * fm), fold(w * w * fm)

    arrived(s["gf"].at[pl.ds(pl.multiple_of(mate * half, half), half)], "gc", 1, mate_peer)
    g_hi, g_lo = parts(s["gf"][...], 2)
    f3 = parts(f, 3)
    e = mxu(f3[0], g_hi, NN) + mxu(f3[0], g_lo, NN) + mxu(f3[1], g_hi, NN) + mxu(f3[1], g_lo, NN) + mxu(f3[2], g_hi, NN)
    fe = f * e
    sum_fe, sum_wfe, sum_qee = fold(fe), fold(w * fe), fold(qw_row * e * e)
    h = w * m + e
    w2 = w * u + dot_l(h * qw_row, qb[...], NT)

    for k in range(1, n_cell):
        arrived(s["exr"].at[k], "ex", k, c_peer(k))
    ex = s["ex"][...]
    for k in range(1, n_cell):
        ex = ex + s["exr"][k]
    nq = queries // 128
    t0q = jnp.concatenate([ex[i : i + 1] for i in range(nq)], axis=1)
    t1q = jnp.concatenate([ex[nq + i : nq + i + 1] for i in range(nq)], axis=1)
    bb, bwb, wbwb, wbwwb, t00, t01, t02, t11 = [ex[2 * nq + i : 2 * nq + i + 1] for i in range(8)]
    zq = t0q * qw_row
    zq8 = jnp.broadcast_to(zq, (8, queries))
    z3 = parts(zq8, 3)
    zg = (mxu(z3[0], g_hi, NN) + mxu(z3[0], g_lo, NN) + mxu(z3[1], g_hi, NN) + mxu(z3[1], g_lo, NN) + mxu(z3[2], g_hi, NN))[0:1]
    t0k = dot_l(zq8, qb[...], NT)[0:1]
    q00, q01, zgz = fold(zq * t0q), fold(zq * t1q), fold(zg * zq)
    t0k2 = jnp.concatenate([t0k[:, :128], t0k[:, 128:]], axis=0)
    sw = t[3:4]
    gs = GROUP_SIZE
    mu0 = bb
    mu1 = bwb + sum_fm + 0.25 * t00
    mu2 = wbwb + 2.0 * sum_wfm + sum_fe + 0.5 * (t01 + q00) + (gs / 16) * t00
    mu3 = (
        (wbwwb + 2.0 * sum_wwfm + sum_wfe)
        + (sum_wwfm + 2.0 * sum_wfe + sum_qee)
        + 0.5 * (t02 + q01)
        + sw * t00 * (1 / 16)
        + 0.5 * (q01 + zgz)
        + (gs / 16) * q00
        + 0.25 * (t11 + (gs / 2) * t01 + (gs * gs / 16) * t00)
        + 0.5 * (q01 + (gs / 4) * q00)
        + 0.25 * zgz
    )
    s["az"][...] = jnp.concatenate(
        [t0, 0.25 * t1 + 0.5 * t0k2 + (gs / 16) * t0, mu0, mu1, mu2, mu3], axis=0
    )
    s["azr"][z] = s["az"][...]
    for k in spread_order(NZ):
        send(s["az"], s["azr"].at[z], "az", k, z_peer(k))
    for k in spread_order(NZ)[::-1]:
        arrived(s["azr"].at[to_z(NZ - k)], "az", k, z_peer(k))
    for i in range(4):
        s["ay"][:, i * 128 : (i + 1) * 128] = s["azr"][:, i, :]
    mu = jnp.sum(s["azr"][...], axis=0)[4:8]
    s["ay"][:, 512:] = jnp.concatenate([mu] + [jnp.zeros_like(mu)] * (NZ // 4 - 1), axis=0)
    for k in spread_order(NY):
        send(s["ay"], s["ayr"].at[y], "ay", k, y_peer(k))
    s["ayr"][y] = s["ay"][...]
    for k in spread_order(NY)[::-1]:
        arrived(s["ayr"].at[to_y(NY - k)], "ay", k, y_peer(k))

    ayr = s["ayr"][...]
    spread = dot_r(pick, ayr[:, :, :512].reshape(groups, 512), NN)
    mu = jnp.sum(jnp.sum(ayr[:, 0:4, 512:], axis=0), axis=1, keepdims=True)
    mu0, mu1, mu2, mu3 = [mu[i : i + 1] for i in range(4)]
    alpha0 = mu0 / mu1
    rr1 = alpha0 * alpha0 * mu2 - mu0
    up = 1.0 + rr1 / mu0
    alpha1 = rr1 / (up * up * mu1 - 2.0 * alpha0 * up * mu2 + alpha0 * alpha0 * mu3)
    c1 = alpha0 + alpha1 * up
    c2 = alpha0 * alpha1
    t0b = spread[:, :cells]
    w1 = u + 0.25 * t0b
    x_out[...] = c1 * b - c2 * w1
    r_out[...] = b - c1 * w1 + c2 * (w2 + 0.25 * (w * t0b) + spread[:, cells:])

    for copy in sends:
        copy.wait_send()


def local(detail_rows, row_block, block_weight, block_group, query_matrix, query_weight, query_noisy, group_noisy):
    blk, cells = detail_rows.shape
    scratch = scratch_of(blk, cells, query_matrix.shape[1], group_noisy.shape[0])
    out = jax.ShapeDtypeStruct((blk, cells), F32)
    return pl.pallas_call(
        functools.partial(kernel, tuple(scratch)),
        out_shape=(out, out),
        in_specs=[pl.BlockSpec(memory_space=pl.ANY)] * 8,
        out_specs=(pl.BlockSpec(memory_space=pltpu.VMEM),) * 2,
        scratch_shapes=list(scratch.values()),
        compiler_params=pltpu.CompilerParams(
            collective_id=0, has_side_effects=True, vmem_limit_bytes=40 * 1024 * 1024
        ),
    )(
        detail_rows,
        row_block.reshape(1, -1),
        block_weight.reshape(1, -1),
        block_group.reshape(1, -1),
        query_matrix,
        query_weight.reshape(1, -1),
        query_noisy,
        group_noisy,
    )


def solution(mesh):
    return jax.shard_map(
        local,
        mesh=mesh,
        in_specs=(
            P("geo", "cell"),
            P("geo"),
            P("geo"),
            P("geo"),
            P("cell", None),
            P(),
            P("geo", None),
            P(None, "cell"),
        ),
        out_specs=(P("geo", "cell"), P("geo", "cell")),
        check_vma=False,
    )
```

time: 917 us -> 67.1 us (0.07)
  waiting for transfers between devices: 502 us -> 0 us
  blocking collectives: 348 us -> 0 us
  Pallas kernels: 0 us -> 59.7 us
  starting transfers between devices: 24.1 us -> 0 us
  between operations: 19.7 us -> 0.68 us
    psum x2 -> x0, waiting for transfers between devices: 477 us -> none  [local(): totals = lax.psum(partial_totals, 'geo')]
    psum x3 -> x0, blocking collectives: 300 us -> none  [the longest x2 200 us: squares(): return lax.psum(jnp.sum(vector * vector), ('geo', 'cell'))]
    pallas_call x0 -> x1, Pallas kernels: none -> 59.7 us  [local(): pl.pallas_call(functools.partial(kernel, tuple(scratch)), out_shape=(out,...]
    all_gather x2 -> x0, blocking collectives: 47.8 us -> none  [local(): lax.all_gather(share_part, 'cell', axis=0, tiled=True)]
    all_to_all x2 -> x0, waiting for transfers between devices: 25.1 us -> none  [the longest x1 13.3 us: local(): lax.all_to_all(detail_rows, 'geo', split_axis=0, concat_axis=0, tiled=True)]
    all_to_all x2 -> x0, starting transfers between devices: 23.9 us -> none  [the longest x1 19.3 us: local(): lax.all_to_all(sent_ids, 'geo', split_axis=0, concat_axis=0, tiled=True)]
  transfers between devices with their start and end apart: 6 -> 0, of which waited for: 4 -> 0; matrix products, arithmetic and copies ran while one was open for 1% -> 0% of each run, Pallas kernels for 0% -> 0%
where the time goes in v1:
time: 67.1 us; the launch traced here: 66.1 us
  Pallas kernels  59.7 us (89%)
  local copies, waits for them, and re-layouts  5.72 us (9%)
  between operations  0.68 us (1%)
    pallas_call x1, Pallas kernels, local(): pl.pallas_call(functools.partial(kernel, tuple(scratch)), out_shape=(out,...  59.7 us
    unnamed x18, local copies, waits for them, and re-layouts  5.72 us

profile of v1, /device:TPU:1, one launch (start us, length us, event | category | flops | bytes accessed | tf_op | source)
XLA Modules:
  0.0 66.1 jit_solution(1597445656778115269)
XLA Ops:
  0.6 0.0 copy-start.4
  0.6 0.0 copy-start.5
  0.7 0.0 copy-start.6
  0.7 0.0 copy-start.7
  0.7 0.6 copy-done.4
  1.3 0.0 copy-done.5
  1.3 0.0 copy-done.6
  1.3 0.0 copy-done.7
  1.3 0.0 copy-start
  1.3 1.0 %copy-done = s32[256,512]{1,0:T(8,128)S(1)} copy-done((s32[256,512]{1,0:T(8,128)S(1)}, s32[256,512]{1,0:T(8,128)}, u32[]{:S(2)}) %copy-start) | copy-done | bytes 524312
  2.4 0.0 copy-start.1
  2.4 0.9 %copy-done.1 = f32[128,512]{1,0:T(8,128)S(1)} copy-done((f32[128,512]{1,0:T(8,128)S(1)}, f32[128,512]{1,0:T(8,128)}, u32[]{:S(2)}) %copy-start.1) | copy-done | bytes 262168
  3.3 0.0 copy-start.2
  3.3 0.9 %copy-done.2 = f32[128,256]{1,0:T(8,128)S(1)} copy-done((f32[128,256]{1,0:T(8,128)S(1)}, f32[128,256]{1,0:T(8,128)}, u32[]{:S(2)}) %copy-start.2) | copy-done | bytes 131096
  4.2 0.0 copy-start.3
  4.2 0.8 %copy-done.3 = f32[64,256]{1,0:T(8,128)S(1)} copy-done((f32[64,256]{1,0:T(8,128)S(1)}, f32[64,256]{1,0:T(8,128)}, u32[]{:S(2)}) %copy-start.3) | copy-done | bytes 65560
  5.1 59.7 %shard_map.95 = (f32[128,256]{1,0:T(8,128)S(1)}, f32[128,256]{1,0:T(8,128)S(1)}) custom-call(f32[128,256]{1,0:T(8,128)S(1)} %copy-done.2, s32[1,128]{1,0:T(1,128)S(1)} %bitcast.5, s32[1,128]{1,0:T(1,128)S(1)} %bitcast.6, s32[1,128]{1,0:T(1,128)S(1)} %bitcast.7, s32[256,512]{1,0:T(8,128)S(1)} %copy-done, f32[1,512]{1,0:T(1,128)S(1)} %bitcast.4, ...), custom_call_target="tpu_custom_call" | custom-call | tf_op jit(solution)/shard_map/pallas_call | solution.py:415
  64.8 0.7 copy.12
  65.5 0.7 copy.13
Async XLA Ops:
  0.6 0.7 %copy-start.4 = (f32[512]{0:T(512)S(1)}, f32[512]{0:T(512)}, u32[]{:S(2)}) copy-start(f32[512]{0:T(512)} %param.13) | copy-start | bytes 6148
  0.6 0.7 %copy-start.5 = (s32[128]{0:T(128)S(1)}, s32[128]{0:T(128)}, u32[]{:S(2)}) copy-start(s32[128]{0:T(128)} %param.9) | copy-start | bytes 1540
  0.7 0.7 %copy-start.6 = (s32[128]{0:T(128)S(1)}, s32[128]{0:T(128)}, u32[]{:S(2)}) copy-start(s32[128]{0:T(128)} %param.10) | copy-start | bytes 1540
  0.7 0.7 %copy-start.7 = (s32[128]{0:T(128)S(1)}, s32[128]{0:T(128)}, u32[]{:S(2)}) copy-start(s32[128]{0:T(128)} %param.11) | copy-start | bytes 1540
  1.3 1.0 %copy-start = (s32[256,512]{1,0:T(8,128)S(1)}, s32[256,512]{1,0:T(8,128)}, u32[]{:S(2)}) copy-start(s32[256,512]{1,0:T(8,128)} %qm.1) | copy-start | bytes 1572868
  2.4 0.9 %copy-start.1 = (f32[128,512]{1,0:T(8,128)S(1)}, f32[128,512]{1,0:T(8,128)}, u32[]{:S(2)}) copy-start(f32[128,512]{1,0:T(8,128)} %qn.1) | copy-start | bytes 786436
  3.3 0.9 %copy-start.2 = (f32[128,256]{1,0:T(8,128)S(1)}, f32[128,256]{1,0:T(8,128)}, u32[]{:S(2)}) copy-start(f32[128,256]{1,0:T(8,128)} %dr.1) | copy-start | bytes 393220
  4.2 0.8 %copy-start.3 = (f32[64,256]{1,0:T(8,128)S(1)}, f32[64,256]{1,0:T(8,128)}, u32[]{:S(2)}) copy-start(f32[64,256]{1,0:T(8,128)} %gn.1) | copy-start | bytes 196612

commit v2 on v1

v2 whole, which is shorter than its diff:
```python
import functools
import jax
import jax.numpy as jnp
from jax import lax
from jax.experimental import pallas as pl
from jax.experimental.pallas import tpu as pltpu
from jax.sharding import PartitionSpec as P

NZ, NY, NX, NC = 16, 4, 4, 2
GROUP_SIZE = 128.0
F32, BF16 = jnp.float32, jnp.bfloat16
NN = (((1,), (0,)), ((), ()))
NT = (((1,), (1,)), ((), ()))
TN = (((0,), (0,)), ((), ()))


def parts(x, n):
    out = []
    for i in range(n):
        p = x.astype(BF16)
        out.append(p)
        if i < n - 1:
            x = x - p.astype(F32)
    return out


def mxu(a, b, dims):
    return lax.dot_general(a, b, dims, preferred_element_type=F32)


def dot_l(x, y, dims, n=3):
    return functools.reduce(lambda s, p: s + p, [mxu(p, y, dims) for p in parts(x, n)])


def dot_r(x, y, dims, n=3):
    return functools.reduce(lambda s, p: s + p, [mxu(x, p, dims) for p in parts(y, n)])


def fold(v):
    s = jnp.sum(v, axis=0, keepdims=True)
    return functools.reduce(
        lambda p, q: p + q, [s[:, i : i + 128] for i in range(0, s.shape[1], 128)]
    )


def spread_order(n):
    return sorted(range(1, n), key=lambda k: -min(k, n - k))


def block_pairs(queries):
    n = queries // 128
    return [(i, j) for i in range(n) for j in range(i, n)]


def scratch_of(blk, cells, queries, groups):
    n_cell = NX * NC
    share = blk // n_cell
    half = len(block_pairs(queries)) * 128 // NC
    hx = half // NX
    zr = blk // NZ
    shapes = {
        "qi": ((cells, queries), jnp.int32),
        "qb": ((cells, queries), BF16),
        "bwv": ((1, blk), jnp.int32),
        "bgv": ((1, blk), jnp.int32),
        "qwv": ((1, queries), F32),
        "qnv": ((blk, queries), F32),
        "gnv": ((groups, cells), F32),
        "ar": ((NZ, zr, cells), F32),
        "ai": ((NZ, 1, blk), jnp.int32),
        "sy": ((NY, zr // NY, NZ, cells), F32),
        "br": ((NY, zr // NY, NZ, cells), F32),
        "bi": ((NY, NZ, 1, blk), jnp.int32),
        "md": ((8, blk), F32),
        "mdr": ((NY, 8, blk), F32),
        "gz": ((groups, NY * blk), BF16),
        "tp": ((groups, 3 * cells), F32),
        "ty": ((NY - 1, NZ, 3 * cells), F32),
        "pz": ((NZ, 8, 128), F32),
        "tz": ((NZ - 1, 8, 128), F32),
        "ex": ((16, 128), F32),
        "exr": ((n_cell - 1, 16, 128), F32),
        "mp": ((blk, queries), F32),
        "mr": ((n_cell - 1, share, queries), F32),
        "ms": ((share, queries), F32),
        "mf": ((blk, queries), F32),
        "gp": ((NC * half, 128), F32),
        "gc": ((half, 128), F32),
        "gh": ((half, 128), F32),
        "gr": ((NX - 1, hx, 128), F32),
        "gs": ((hx, 128), F32),
        "gf": ((NC * half, 128), F32),
        "g_hi": ((queries, queries), BF16),
        "g_lo": ((queries, queries), BF16),
        "az": ((4, 128), F32),
        "azr": ((NZ, 4, 128), F32),
        "ay": ((NZ, 512), F32),
        "ayr": ((NY, NZ, 512), F32),
        "mz": ((4, 128), F32),
        "mzr": ((NZ, 4, 128), F32),
        "my": ((4, 128), F32),
        "myr": ((NY, 4, 128), F32),
        "base": ((blk, cells), F32),
        "bv": ((blk, cells), F32),
        "uv": ((blk, cells), F32),
        "w2l": ((blk, cells), F32),
        "w1v": ((blk, cells), F32),
        "w2v": ((blk, cells), F32),
        "cv": ((8, cells), F32),
    }
    dma = pltpu.SemaphoreType.DMA
    out = {k: pltpu.VMEM(*v) for k, v in shapes.items()}
    out["load"] = dma((6,))
    out["out"] = dma((4,))
    for name in PHASES:
        out[name + "_s"] = dma
        out[name + "_r"] = dma
    return out


PHASES = ("z", "zi", "y", "yi", "md", "ty", "tz", "ex", "mr", "ma", "gc", "gd", "gr", "ga", "az", "ay", "mz", "my")


def kernel(names, dr, rb, bw, bg, qm, qw, qn, gn, b_out, w1_out, w2_out, c_out, *refs):
    s = dict(zip(names, refs))
    blk, cells = dr.shape
    queries = qm.shape[1]
    groups = gn.shape[0]
    n_cell = NX * NC
    zr = blk // NZ
    sr = zr // NY
    share = blk // n_cell
    half = len(block_pairs(queries)) * 128 // NC
    hx = half // NX
    geo = lax.axis_index("geo")
    cell = lax.axis_index("cell")
    z, y = geo // NY, lax.rem(geo, NY)
    x, core = cell // NC, lax.rem(cell, NC)
    mate = 1 - core

    def to_z(k):
        return lax.rem(z + k, NZ)

    def to_y(k):
        return lax.rem(y + k, NY)

    def to_x(k):
        return lax.rem(x + k, NX)

    def to_c(k):
        return lax.rem(cell + k, n_cell)

    def z_peer(k):
        return (to_z(k) * NY + y, cell)

    def y_peer(k):
        return (z * NY + to_y(k), cell)

    def x_peer(k):
        return (geo, to_x(k) * NC + core)

    def c_peer(k):
        return (geo, to_c(k))

    mate_peer = (geo, x * NC + mate)

    def rows(i, n):
        return pl.ds(pl.multiple_of(i * n, n), n)

    def send(src, dst, name, peer):
        pltpu.make_async_remote_copy(
            src_ref=src,
            dst_ref=dst,
            send_sem=s[name + "_s"],
            recv_sem=s[name + "_r"],
            device_id=peer,
            device_id_type=pl.DeviceIdType.MESH,
        ).start()

    def keep(src, dst, name):
        pltpu.make_async_copy(src, dst, s[name + "_r"]).start()

    def arrived(ref, name):
        pltpu.make_async_copy(ref, ref, s[name + "_r"]).wait()

    def sent(ref, name):
        pltpu.make_async_copy(ref, ref, s[name + "_s"]).wait()

    barrier = pltpu.get_barrier_semaphore()
    greet = (
        [z_peer(k) for k in spread_order(NZ)]
        + [y_peer(k) for k in range(1, NY)]
        + [c_peer(k) for k in range(1, n_cell)]
    )
    for peer in greet:
        pl.semaphore_signal(barrier, inc=1, device_id=peer, device_id_type=pl.DeviceIdType.MESH)
    loads = [
        pltpu.make_async_copy(src, s[dst], s["load"].at[i])
        for i, (src, dst) in enumerate([(qm, "qi"), (bw, "bwv"), (bg, "bgv"), (qw, "qwv"), (qn, "qnv"), (gn, "gnv")])
    ]
    for copy in loads:
        copy.start()
    keep(dr.at[rows(z, zr)], s["ar"].at[z], "z")
    keep(rb, s["ai"].at[z], "zi")

    loads[0].wait()
    qb = s["qb"]
    qb[...] = s["qi"][...].astype(F32).astype(BF16)
    pairs = block_pairs(queries)
    at = 0
    for i in range(queries // 128):
        strip = mxu(qb[:, i * 128 : (i + 1) * 128], qb[:, i * 128 :], TN)
        for j in range(0, strip.shape[1], 128):
            s["gp"][at : at + 128] = strip[:, j : j + 128]
            at += 128
    loads[1].wait()
    loads[2].wait()
    w_row = s["bwv"][...].astype(F32)
    bg_row = s["bgv"][...].astype(F32)
    s["md"][...] = jnp.concatenate([w_row, bg_row] + [jnp.zeros_like(w_row)] * 6, axis=0)
    pl.semaphore_wait(barrier, len(greet))

    for k in spread_order(NZ):
        send(dr.at[rows(to_z(k), zr)], s["ar"].at[z], "z", z_peer(k))
        send(rb, s["ai"].at[z], "zi", z_peer(k))
    for k in spread_order(NY):
        send(s["md"], s["mdr"].at[y], "md", y_peer(k))
    keep(s["md"], s["mdr"].at[y], "md")
    send(s["gp"].at[rows(mate, half)], s["gc"], "gc", mate_peer)

    for copy in loads[3:]:
        copy.wait()
    eye = lax.broadcasted_iota(jnp.int32, (blk, blk), 0) == lax.broadcasted_iota(jnp.int32, (blk, blk), 1)
    w = jnp.sum(jnp.where(eye, w_row, 0.0), axis=1, keepdims=True)
    bg_col = jnp.sum(jnp.where(eye, bg_row, 0.0), axis=1, keepdims=True)
    pick = (bg_col == lax.broadcasted_iota(jnp.int32, (blk, groups), 1).astype(F32)).astype(F32).astype(BF16)
    gather = (bg_row == lax.broadcasted_iota(jnp.int32, (groups, blk), 0).astype(F32)).astype(F32).astype(BF16)
    qw_row = s["qwv"][...]
    base = dot_l(s["qnv"][...] * qw_row, qb[...], NT) + 0.25 * dot_r(pick, s["gnv"][...], NN)
    s["base"][...] = base
    s["tp"][...] = dot_r(gather, jnp.concatenate([base, w * base, w * w * base], axis=1), NN)

    arrived(s["gc"], "gc")
    s["gh"][...] = s["gp"][rows(core, half)] + s["gc"][...]
    for k in spread_order(NX):
        send(s["gh"].at[rows(to_x(k), hx)], s["gr"].at[k - 1], "gr", x_peer(k))

    arrived(s["mdr"], "md")
    w_all = jnp.concatenate([s["mdr"][i, 0:1] for i in range(NY)], axis=1)
    bg_all = jnp.concatenate([s["mdr"][i, 1:2] for i in range(NY)], axis=1)
    s["gz"][...] = (
        bg_all == lax.broadcasted_iota(jnp.int32, (groups, NY * blk), 0).astype(F32)
    ).astype(F32).astype(BF16)
    mine = bg_all == (lax.broadcasted_iota(jnp.int32, (NZ, NY * blk), 0) + y * NZ).astype(F32)
    s["pz"][:, 3, :] = jnp.broadcast_to(jnp.sum(jnp.where(mine, w_all, 0.0), axis=1, keepdims=True), (NZ, 128))
    s["pz"][:, 7, :] = jnp.zeros((NZ, 128), F32)

    arrived(s["ar"], "z")
    arrived(s["ai"], "zi")
    for yy in range(NY):
        for kk in range(sr):
            s["sy"][yy, kk] = s["ar"][:, yy * sr + kk, :]
    for k in spread_order(NY):
        send(s["sy"].at[to_y(k)], s["br"].at[y], "y", y_peer(k))
        send(s["ai"], s["bi"].at[y], "yi", y_peer(k))
    keep(s["sy"].at[y], s["br"].at[y], "y")
    keep(s["ai"], s["bi"].at[y], "yi")

    ids = s["ai"][...].reshape(NZ, blk).astype(F32)
    lane = lax.broadcasted_iota(jnp.int32, (NZ, blk), 1)
    id_col = jnp.concatenate(
        [jnp.sum(jnp.where(lane == z * zr + j, ids, 0.0), axis=1, keepdims=True) for j in range(zr)], axis=0
    )
    spot = lax.broadcasted_iota(jnp.int32, (blk, NY * blk), 1) + z * (NY * blk)
    is_at = id_col == spot.astype(F32)
    wr = jnp.sum(jnp.where(is_at, w_all, 0.0), axis=1, keepdims=True)
    of_row = mxu(s["gz"][...], is_at.astype(F32).astype(BF16), NT).astype(BF16)
    r1 = wr * s["sy"][...].reshape(blk, cells)
    r2 = wr * r1
    s["tp"][...] += dot_r(of_row, jnp.concatenate([r1, r2, wr * r2], axis=1), NN)
    for k in spread_order(NY):
        send(s["tp"].at[rows(to_y(k), NZ)], s["ty"].at[k - 1], "ty", y_peer(k))

    arrived(s["gr"], "gr")
    total = s["gh"][rows(x, hx)]
    for k in range(NX - 1):
        total = total + s["gr"][k]
    s["gs"][...] = total
    spot_g = pl.ds(pl.multiple_of(core * half + x * hx, hx), hx)
    for k in spread_order(NX):
        send(s["gs"], s["gf"].at[spot_g], "ga", x_peer(k))
    keep(s["gs"], s["gf"].at[spot_g], "ga")

    arrived(s["br"], "y")
    arrived(s["bi"], "yi")
    ids = s["bi"][...].reshape(NY * NZ, blk).astype(F32)
    lane = lax.broadcasted_iota(jnp.int32, (NY * NZ, blk), 1)
    id_col = jnp.concatenate(
        [
            jnp.sum(jnp.where(lane == geo * sr + kk, ids, 0.0), axis=1, keepdims=True)
            for kk in range(sr)
        ],
        axis=0,
    )
    moved = jnp.concatenate([s["br"][:, kk].reshape(NY * NZ, cells) for kk in range(sr)], axis=0)
    here = lax.broadcasted_iota(jnp.int32, (blk, blk), 1) + geo * blk
    place = (id_col == here.astype(F32)).astype(F32).astype(BF16)
    b = w * dot_r(place, moved, TN) + s["base"][...]
    s["bv"][...] = b
    outs = [pltpu.make_async_copy(s["bv"], b_out, s["out"].at[0])]
    outs[0].start()
    s["mp"][...] = dot_l(b, qb[...], NN)
    for k in range(1, n_cell):
        send(s["mp"].at[rows(to_c(k), share)], s["mr"].at[k - 1], "mr", c_peer(k))

    arrived(s["ty"], "ty")
    t = s["tp"][rows(y, NZ)]
    for k in range(NY - 1):
        t = t + s["ty"][k]
    for i, row in enumerate([0, 4, 1, 5, 2, 6]):
        s["pz"][:, row, :] = t[:, i * 128 : (i + 1) * 128]
    for k in spread_order(NZ):
        send(s["pz"].at[to_z(k)], s["tz"].at[k - 1], "tz", z_peer(k))

    wb = w * b
    scal_b = [fold(b * b), fold(b * wb), fold(wb * wb), fold(wb * (w * wb))]

    arrived(s["mr"], "mr")
    m_own = s["mp"][rows(cell, share)]
    for k in range(n_cell - 1):
        m_own = m_own + s["mr"][k]
    s["ms"][...] = m_own

    held = s["gf"].at[rows(core, half)]
    arrived(held, "ga")
    send(held, held, "gd", mate_peer)

    arrived(s["tz"], "tz")
    t = s["pz"][z]
    for k in range(NZ - 1):
        t = t + s["tz"][k]
    q0 = dot_l(t, qb[:128], NN)
    q1 = dot_l(t, qb[128:], NN)
    tq = q0[0:2] + q1[4:6]
    t0, t1, t2 = [jnp.concatenate([t[i : i + 1], t[i + 4 : i + 5]], axis=0) for i in range(3)]
    s["ex"][...] = jnp.concatenate(
        [tq[i : i + 1, j : j + 128] for i in range(2) for j in range(0, queries, 128)]
        + scal_b
        + [fold(t0 * t0), fold(t0 * t1), fold(t0 * t2), fold(t1 * t1)],
        axis=0,
    )
    for k in range(1, n_cell):
        send(s["ex"], s["exr"].at[k - 1], "ex", c_peer(k))

    for k in range(1, n_cell):
        send(s["ms"], s["mf"].at[rows(cell, share)], "ma", c_peer(k))
    keep(s["ms"], s["mf"].at[rows(cell, share)], "ma")

    arrived(s["gf"].at[rows(mate, half)], "gd")
    for n, (i, j) in enumerate(pairs):
        block = s["gf"][n * 128 : (n + 1) * 128]
        for r, c, v in ((i, j, block), (j, i, block.T))[: 1 + (i < j)]:
            spot = (slice(r * 128, (r + 1) * 128), slice(c * 128, (c + 1) * 128))
            s["g_hi"][spot], s["g_lo"][spot] = parts(v, 2)

    def gram(v):
        p = parts(v, 3)
        hi, lo = s["g_hi"][...], s["g_lo"][...]
        return mxu(p[0], hi, NN) + mxu(p[0], lo, NN) + mxu(p[1], hi, NN) + mxu(p[1], lo, NN) + mxu(p[2], hi, NN)

    arrived(s["exr"], "ex")
    ex = s["ex"][...]
    for k in range(n_cell - 1):
        ex = ex + s["exr"][k]
    nq = queries // 128
    t0q = jnp.concatenate([ex[i : i + 1] for i in range(nq)], axis=1)
    t1q = jnp.concatenate([ex[nq + i : nq + i + 1] for i in range(nq)], axis=1)
    bb, bwb, wbwb, wbwwb, t00, t01, t02, t11 = [ex[2 * nq + i : 2 * nq + i + 1] for i in range(8)]
    zq = t0q * qw_row
    zq8 = jnp.broadcast_to(zq, (8, queries))
    t0k = dot_l(zq8, qb[...], NT)[0:1]
    t0k2 = jnp.concatenate([t0k[:, :128], t0k[:, 128:]], axis=0)
    gs = GROUP_SIZE
    s["az"][...] = jnp.concatenate([t0, 0.25 * t1 + 0.5 * t0k2 + (gs / 16) * t0], axis=0)
    for k in spread_order(NZ):
        send(s["az"], s["azr"].at[z], "az", z_peer(k))
    keep(s["az"], s["azr"].at[z], "az")

    arrived(s["mf"], "ma")
    zg = gram(zq8)[0:1]
    q00, q01, zgz = fold(zq * t0q), fold(zq * t1q), fold(zg * zq)
    sw = t[3:4]
    m = s["mf"][...]
    f = m * qw_row
    fm = f * m
    sum_fm, sum_wfm, sum_wwfm = fold(fm), fold(w * fm), fold(w * w * fm)
    e = gram(f)
    fe = f * e
    sum_fe, sum_wfe, sum_qee = fold(fe), fold(w * fe), fold(qw_row * e * e)
    mu0 = bb
    mu1 = bwb + sum_fm + 0.25 * t00
    mu2 = wbwb + 2.0 * sum_wfm + sum_fe + 0.5 * (t01 + q00) + (gs / 16) * t00
    mu3 = (
        (wbwwb + 2.0 * sum_wwfm + sum_wfe)
        + (sum_wwfm + 2.0 * sum_wfe + sum_qee)
        + 0.5 * (t02 + q01)
        + sw * t00 * (1 / 16)
        + 0.5 * (q01 + zgz)
        + (gs / 16) * q00
        + 0.25 * (t11 + (gs / 2) * t01 + (gs * gs / 16) * t00)
        + 0.5 * (q01 + (gs / 4) * q00)
        + 0.25 * zgz
    )
    s["mz"][...] = jnp.concatenate([mu0, mu1, mu2, mu3], axis=0)
    for k in spread_order(NZ):
        send(s["mz"], s["mzr"].at[z], "mz", z_peer(k))
    keep(s["mz"], s["mzr"].at[z], "mz")
    u = w * s["bv"][...] + dot_l(f, qb[...], NT)
    s["uv"][...] = u
    s["w2l"][...] = w * u + dot_l((w * m + e) * qw_row, qb[...], NT)

    arrived(s["azr"], "az")
    for i in range(4):
        s["ay"][:, i * 128 : (i + 1) * 128] = s["azr"][:, i, :]
    for k in spread_order(NY):
        send(s["ay"], s["ayr"].at[y], "ay", y_peer(k))
    keep(s["ay"], s["ayr"].at[y], "ay")
    arrived(s["mzr"], "mz")
    s["my"][...] = jnp.sum(s["mzr"][...], axis=0)
    for k in spread_order(NY):
        send(s["my"], s["myr"].at[y], "my", y_peer(k))
    keep(s["my"], s["myr"].at[y], "my")
    arrived(s["ayr"], "ay")
    spread = dot_r(pick, s["ayr"][...].reshape(groups, 512), NN)
    t0b = spread[:, :cells]
    s["w1v"][...] = s["uv"][...] + 0.25 * t0b
    s["w2v"][...] = s["w2l"][...] + (0.25 * (w * t0b) + spread[:, cells:])
    outs += [
        pltpu.make_async_copy(s["w1v"], w1_out, s["out"].at[1]),
        pltpu.make_async_copy(s["w2v"], w2_out, s["out"].at[2]),
    ]
    outs[1].start()
    outs[2].start()
    arrived(s["myr"], "my")
    mu = jnp.sum(jnp.sum(s["myr"][...], axis=0), axis=1, keepdims=True)
    mu0, mu1, mu2, mu3 = [mu[i : i + 1] for i in range(4)]
    alpha0 = mu0 / mu1
    rr1 = alpha0 * alpha0 * mu2 - mu0
    up = 1.0 + rr1 / mu0
    alpha1 = rr1 / (up * up * mu1 - 2.0 * alpha0 * up * mu2 + alpha0 * alpha0 * mu3)
    c1 = alpha0 + alpha1 * up
    c2 = alpha0 * alpha1
    s["cv"][...] = jnp.concatenate([jnp.broadcast_to(c, (4, cells)) for c in (c1, c2)], axis=0)
    outs.append(pltpu.make_async_copy(s["cv"], c_out, s["out"].at[3]))
    outs[3].start()

    for name, ref in (
        ("z", s["ar"].at[: NZ - 1]),
        ("zi", s["ai"].at[: NZ - 1]),
        ("y", s["br"].at[: NY - 1]),
        ("yi", s["bi"].at[: NY - 1]),
        ("md", s["mdr"].at[: NY - 1]),
        ("ty", s["ty"]),
        ("tz", s["tz"]),
        ("ex", s["exr"]),
        ("mr", s["mr"]),
        ("ma", s["mr"]),
        ("gc", s["gc"]),
        ("gd", s["gc"]),
        ("gr", s["gr"]),
        ("ga", s["gr"]),
        ("az", s["azr"].at[: NZ - 1]),
        ("ay", s["ayr"].at[: NY - 1]),
        ("mz", s["mzr"].at[: NZ - 1]),
        ("my", s["myr"].at[: NY - 1]),
    ):
        sent(ref, name)
    for copy in outs:
        copy.wait()


def combine(b_in, w1_in, w2_in, c_in, x_out, r_out, b, w1, w2, c, x, r, load, load_c, store):
    blk = b.shape[0]
    steps = store.shape[0]
    n = blk // steps
    get_c = pltpu.make_async_copy(c_in, c, load_c)
    get_c.start()
    gets, puts = [], []
    for i in range(steps):
        part = pl.ds(i * n, n)
        gets.append(
            [
                pltpu.make_async_copy(src.at[part], dst.at[part], load.at[i, j])
                for j, (src, dst) in enumerate(((b_in, b), (w1_in, w1), (w2_in, w2)))
            ]
        )
        for copy in gets[-1]:
            copy.start()
    get_c.wait()
    c1, c2 = c[0:1], c[4:5]
    for i in range(steps):
        part = pl.ds(i * n, n)
        for copy in gets[i]:
            copy.wait()
        x[part] = c1 * b[part] - c2 * w1[part]
        r[part] = b[part] - c1 * w1[part] + c2 * w2[part]
        for j, (src, dst) in enumerate(((x, x_out), (r, r_out))):
            puts.append(pltpu.make_async_copy(src.at[part], dst.at[part], store.at[i, j]))
            puts[-1].start()
    for copy in puts:
        copy.wait()


def local(detail_rows, row_block, block_weight, block_group, query_matrix, query_weight, query_noisy, group_noisy):
    blk, cells = detail_rows.shape
    scratch = scratch_of(blk, cells, query_matrix.shape[1], group_noisy.shape[0])
    out = jax.ShapeDtypeStruct((blk, cells), F32)
    taken = pl.pallas_call(
        functools.partial(kernel, tuple(scratch)),
        out_shape=(out, out, out, jax.ShapeDtypeStruct((8, cells), F32)),
        in_specs=[pl.BlockSpec(memory_space=pl.ANY)] * 8,
        out_specs=(pl.BlockSpec(memory_space=pl.ANY),) * 4,
        scratch_shapes=list(scratch.values()),
        compiler_params=pltpu.CompilerParams(
            collective_id=0, has_side_effects=True, vmem_limit_bytes=60 * 1024 * 1024
        ),
    )(
        detail_rows,
        row_block.reshape(1, -1),
        block_weight.reshape(1, -1),
        block_group.reshape(1, -1),
        query_matrix,
        query_weight.reshape(1, -1),
        query_noisy,
        group_noisy,
    )
    return pl.pallas_call(
        combine,
        out_shape=(out, out),
        in_specs=[pl.BlockSpec(memory_space=pl.ANY)] * 4,
        out_specs=(pl.BlockSpec(memory_space=pl.ANY),) * 2,
        scratch_shapes=[pltpu.VMEM((blk, cells), F32)] * 3
        + [pltpu.VMEM((8, cells), F32)]
        + [pltpu.VMEM((blk, cells), F32)] * 2
        + [pltpu.SemaphoreType.DMA((4, 3)), pltpu.SemaphoreType.DMA, pltpu.SemaphoreType.DMA((4, 2))],
        compiler_params=pltpu.CompilerParams(vmem_limit_bytes=60 * 1024 * 1024),
    )(*taken)


def solution(mesh):
    return jax.shard_map(
        local,
        mesh=mesh,
        in_specs=(
            P("geo", "cell"),
            P("geo"),
            P("geo"),
            P("geo"),
            P("cell", None),
            P(),
            P("geo", None),
            P(None, "cell"),
        ),
        out_specs=(P("geo", "cell"), P("geo", "cell")),
        check_vma=False,
    )
```

time: 67.1 us -> 57.4 us (0.86); the launches traced: 66.1 us -> 57.1 us
  local copies, waits for them, and re-layouts: 5.72 us -> 0 us
  Pallas kernels: 59.7 us -> 56.5 us
    unnamed x18 -> x0, local copies, waits for them, and re-layouts: 5.72 us -> none
    pallas_call x1, Pallas kernels: 59.7 us -> 54.7 us  [local(): pl.pallas_call(functools.partial(kernel, tuple(scratch)), out_shape=(out,...]
    pallas_call x0 -> x1, Pallas kernels: none -> 1.76 us  [local(): pl.pallas_call(combine, out_shape=(out, out), in_specs=[pl.BlockSpec(memo...]
where the time goes in v2:
time: 57.4 us; the launch traced here: 57.1 us
  Pallas kernels  56.5 us (98%)
  between operations  0.64 us (1%)
    pallas_call x1, Pallas kernels, local(): pl.pallas_call(functools.partial(kernel, tuple(scratch)), out_shape=(out,...  54.7 us
    pallas_call x1, Pallas kernels, local(): pl.pallas_call(combine, out_shape=(out, out), in_specs=[pl.BlockSpec(memo...  1.76 us

profile of v2, /device:TPU:1, one launch (start us, length us, event | category | flops | bytes accessed | tf_op | source)
XLA Modules:
  0.0 57.1 jit_solution(11655809590336209151)
XLA Ops:
  0.6 54.7 %shard_map.95 = (f32[128,256]{1,0:T(8,128)}, f32[128,256]{1,0:T(8,128)}, f32[128,256]{1,0:T(8,128)}, f32[8,256]{1,0:T(8,128)}) custom-call(f32[128,256]{1,0:T(8,128)} %dr.1, s32[1,128]{1,0:T(1,128)} %bitcast.5, s32[1,128]{1,0:T(1,128)} %bitcast.6, s32[1,128]{1,0:T(1,128)} %bitcast.7, s32[256,512]{1,0:T(8,128)} %qm.1, f32[1,512]{1,0:T(1,128)} %bitcast.4, ...), custom_call_target="tpu_custom_call" | custom-call | tf_op jit(solution)/shard_map/pallas_call | solution.py:518
  55.4 1.8 %shard_map.96 = (f32[128,256]{1,0:T(8,128)}, f32[128,256]{1,0:T(8,128)}) custom-call(f32[128,256]{1,0:T(8,128)} %get-tuple-element.6.b_in, f32[128,256]{1,0:T(8,128)} %get-tuple-element.7.w1_in, f32[128,256]{1,0:T(8,128)} %get-tuple-element.8.w2_in, f32[8,256]{1,0:T(8,128)} %get-tuple-element.9.c_in), custom_call_target="tpu_custom_call" | custom-call | tf_op jit(solution)/shard_map/pallas_call | solution.py:537

commit v3 on v2

--- a/solution.py
+++ b/solution.py
@@ -36,6 +36,16 @@
     return functools.reduce(lambda s, p: s + p, [mxu(x, p, dims) for p in parts(y, n)])
 
 
+def stack(x):
+    terms = [p.astype(F32) for p in parts(x, 3)]
+    pad = -3 * x.shape[0] % 16
+    return jnp.concatenate(terms + [jnp.zeros((pad, x.shape[1]), F32)] * (pad > 0), axis=0).astype(BF16)
+
+
+def unstack(y, n):
+    return y[:n] + y[n : 2 * n] + y[2 * n : 3 * n]
+
+
 def fold(v):
     s = jnp.sum(v, axis=0, keepdims=True)
     return functools.reduce(
@@ -60,6 +70,8 @@
     zr = blk // NZ
     shapes = {
         "qi": ((cells, queries), jnp.int32),
+        "drv": ((blk, cells), F32),
+        "rbv": ((1, blk), jnp.int32),
         "qb": ((cells, queries), BF16),
         "bwv": ((1, blk), jnp.int32),
         "bgv": ((1, blk), jnp.int32),
@@ -73,7 +85,7 @@
         "bi": ((NY, NZ, 1, blk), jnp.int32),
         "md": ((8, blk), F32),
         "mdr": ((NY, 8, blk), F32),
-        "gz": ((groups, NY * blk), BF16),
+        "gz": ((4 * groups, NY * blk), BF16),
         "tp": ((groups, 3 * cells), F32),
         "ty": ((NY - 1, NZ, 3 * cells), F32),
         "pz": ((NZ, 8, 128), F32),
@@ -94,8 +106,7 @@
         "g_lo": ((queries, queries), BF16),
         "az": ((4, 128), F32),
         "azr": ((NZ, 4, 128), F32),
-        "ay": ((NZ, 512), F32),
-        "ayr": ((NY, NZ, 512), F32),
+        "ayr": ((NY, NZ, 4, 128), F32),
         "mz": ((4, 128), F32),
         "mzr": ((NZ, 4, 128), F32),
         "my": ((4, 128), F32),
@@ -106,22 +117,26 @@
         "w2l": ((blk, cells), F32),
         "w1v": ((blk, cells), F32),
         "w2v": ((blk, cells), F32),
-        "cv": ((8, cells), F32),
+        "xv": ((blk, cells), F32),
+        "rv": ((blk, cells), F32),
     }
     dma = pltpu.SemaphoreType.DMA
     out = {k: pltpu.VMEM(*v) for k, v in shapes.items()}
-    out["load"] = dma((6,))
-    out["out"] = dma((4,))
+    out["load"] = dma((8,))
+    out["out"] = dma((4, 2))
     for name in PHASES:
         out[name + "_s"] = dma
         out[name + "_r"] = dma
     return out
 
 
-PHASES = ("z", "zi", "y", "yi", "md", "ty", "tz", "ex", "mr", "ma", "gc", "gd", "gr", "ga", "az", "ay", "mz", "my")
-
-
-def kernel(names, dr, rb, bw, bg, qm, qw, qn, gn, b_out, w1_out, w2_out, c_out, *refs):
+PHASES = ("z", "zi", "y", "yi", "md", "ty", "tz", "ex", "mr", "ma", "gc", "gd", "gr", "ga", "az", "af", "ay", "mz", "my")
+
+
+FAR = [k for k in range(1, NZ) if min(k, NZ - k) > 5]
+
+
+def kernel(names, dr, rb, bw, bg, qm, qw, qn, gn, x_out, r_out, *refs):
     s = dict(zip(names, refs))
     blk, cells = dr.shape
     queries = qm.shape[1]
@@ -196,14 +211,14 @@
         pl.semaphore_signal(barrier, inc=1, device_id=peer, device_id_type=pl.DeviceIdType.MESH)
     loads = [
         pltpu.make_async_copy(src, s[dst], s["load"].at[i])
-        for i, (src, dst) in enumerate([(qm, "qi"), (bw, "bwv"), (bg, "bgv"), (qw, "qwv"), (qn, "qnv"), (gn, "gnv")])
+        for i, (src, dst) in enumerate([(dr, "drv"), (rb, "rbv"), (qm, "qi"), (bw, "bwv"), (bg, "bgv"), (qw, "qwv"), (qn, "qnv"), (gn, "gnv")])
     ]
     for copy in loads:
         copy.start()
     keep(dr.at[rows(z, zr)], s["ar"].at[z], "z")
     keep(rb, s["ai"].at[z], "zi")
 
-    loads[0].wait()
+    loads[2].wait()
     qb = s["qb"]
     qb[...] = s["qi"][...].astype(F32).astype(BF16)
     pairs = block_pairs(queries)
@@ -213,22 +228,24 @@
         for j in range(0, strip.shape[1], 128):
             s["gp"][at : at + 128] = strip[:, j : j + 128]
             at += 128
-    loads[1].wait()
-    loads[2].wait()
+    loads[3].wait()
+    loads[4].wait()
     w_row = s["bwv"][...].astype(F32)
     bg_row = s["bgv"][...].astype(F32)
     s["md"][...] = jnp.concatenate([w_row, bg_row] + [jnp.zeros_like(w_row)] * 6, axis=0)
+    loads[0].wait()
+    loads[1].wait()
     pl.semaphore_wait(barrier, len(greet))
 
     for k in spread_order(NZ):
-        send(dr.at[rows(to_z(k), zr)], s["ar"].at[z], "z", z_peer(k))
-        send(rb, s["ai"].at[z], "zi", z_peer(k))
+        send(s["drv"].at[rows(to_z(k), zr)], s["ar"].at[z], "z", z_peer(k))
+        send(s["rbv"], s["ai"].at[z], "zi", z_peer(k))
     for k in spread_order(NY):
         send(s["md"], s["mdr"].at[y], "md", y_peer(k))
     keep(s["md"], s["mdr"].at[y], "md")
     send(s["gp"].at[rows(mate, half)], s["gc"], "gc", mate_peer)
 
-    for copy in loads[3:]:
+    for copy in loads[5:]:
         copy.wait()
     eye = lax.broadcasted_iota(jnp.int32, (blk, blk), 0) == lax.broadcasted_iota(jnp.int32, (blk, blk), 1)
     w = jnp.sum(jnp.where(eye, w_row, 0.0), axis=1, keepdims=True)
@@ -248,9 +265,10 @@
     arrived(s["mdr"], "md")
     w_all = jnp.concatenate([s["mdr"][i, 0:1] for i in range(NY)], axis=1)
     bg_all = jnp.concatenate([s["mdr"][i, 1:2] for i in range(NY)], axis=1)
-    s["gz"][...] = (
-        bg_all == lax.broadcasted_iota(jnp.int32, (groups, NY * blk), 0).astype(F32)
-    ).astype(F32).astype(BF16)
+    is_in = bg_all == lax.broadcasted_iota(jnp.int32, (groups, NY * blk), 0).astype(F32)
+    cube = parts(w_all * w_all * w_all, 2)
+    for i, v in enumerate([w_all, w_all * w_all, cube[0].astype(F32), cube[1].astype(F32)]):
+        s["gz"][i * groups : (i + 1) * groups] = jnp.where(is_in, v, 0.0).astype(BF16)
     mine = bg_all == (lax.broadcasted_iota(jnp.int32, (NZ, NY * blk), 0) + y * NZ).astype(F32)
     s["pz"][:, 3, :] = jnp.broadcast_to(jnp.sum(jnp.where(mine, w_all, 0.0), axis=1, keepdims=True), (NZ, 128))
     s["pz"][:, 7, :] = jnp.zeros((NZ, 128), F32)
@@ -273,11 +291,11 @@
     )
     spot = lax.broadcasted_iota(jnp.int32, (blk, NY * blk), 1) + z * (NY * blk)
     is_at = id_col == spot.astype(F32)
-    wr = jnp.sum(jnp.where(is_at, w_all, 0.0), axis=1, keepdims=True)
     of_row = mxu(s["gz"][...], is_at.astype(F32).astype(BF16), NT).astype(BF16)
-    r1 = wr * s["sy"][...].reshape(blk, cells)
-    r2 = wr * r1
-    s["tp"][...] += dot_r(of_row, jnp.concatenate([r1, r2, wr * r2], axis=1), NN)
+    sums = dot_r(of_row, s["sy"][...].reshape(blk, cells), NN)
+    s["tp"][:, :cells] += sums[:groups]
+    s["tp"][:, cells : 2 * cells] += sums[groups : 2 * groups]
+    s["tp"][:, 2 * cells :] += sums[2 * groups : 3 * groups] + sums[3 * groups :]
     for k in spread_order(NY):
         send(s["tp"].at[rows(to_y(k), NZ)], s["ty"].at[k - 1], "ty", y_peer(k))
 
@@ -307,8 +325,6 @@
     place = (id_col == here.astype(F32)).astype(F32).astype(BF16)
     b = w * dot_r(place, moved, TN) + s["base"][...]
     s["bv"][...] = b
-    outs = [pltpu.make_async_copy(s["bv"], b_out, s["out"].at[0])]
-    outs[0].start()
     s["mp"][...] = dot_l(b, qb[...], NN)
     for k in range(1, n_cell):
         send(s["mp"].at[rows(to_c(k), share)], s["mr"].at[k - 1], "mr", c_peer(k))
@@ -330,6 +346,9 @@
     for k in range(n_cell - 1):
         m_own = m_own + s["mr"][k]
     s["ms"][...] = m_own
+    for k in range(1, n_cell):
+        send(s["ms"], s["mf"].at[rows(cell, share)], "ma", c_peer(k))
+    keep(s["ms"], s["mf"].at[rows(cell, share)], "ma")
 
     held = s["gf"].at[rows(core, half)]
     arrived(held, "ga")
@@ -339,9 +358,7 @@
     t = s["pz"][z]
     for k in range(NZ - 1):
         t = t + s["tz"][k]
-    q0 = dot_l(t, qb[:128], NN)
-    q1 = dot_l(t, qb[128:], NN)
-    tq = q0[0:2] + q1[4:6]
+    tq = unstack(mxu(stack(jnp.concatenate([t[0:2], t[4:6]], axis=1)), qb[...], NN), 2)
     t0, t1, t2 = [jnp.concatenate([t[i : i + 1], t[i + 4 : i + 5]], axis=0) for i in range(3)]
     s["ex"][...] = jnp.concatenate(
         [tq[i : i + 1, j : j + 128] for i in range(2) for j in range(0, queries, 128)]
@@ -352,10 +369,6 @@
     for k in range(1, n_cell):
         send(s["ex"], s["exr"].at[k - 1], "ex", c_peer(k))
 
-    for k in range(1, n_cell):
-        send(s["ms"], s["mf"].at[rows(cell, share)], "ma", c_peer(k))
-    keep(s["ms"], s["mf"].at[rows(cell, share)], "ma")
-
     arrived(s["gf"].at[rows(mate, half)], "gd")
     for n, (i, j) in enumerate(pairs):
         block = s["gf"][n * 128 : (n + 1) * 128]
@@ -368,6 +381,14 @@
         hi, lo = s["g_hi"][...], s["g_lo"][...]
         return mxu(p[0], hi, NN) + mxu(p[0], lo, NN) + mxu(p[1], hi, NN) + mxu(p[1], lo, NN) + mxu(p[2], hi, NN)
 
+    arrived(s["mf"], "ma")
+    m = s["mf"][...]
+    f = m * qw_row
+    fm = f * m
+    sum_fm, sum_wfm, sum_wwfm = fold(fm), fold(w * fm), fold(w * w * fm)
+    e = gram(f)
+    fe = f * e
+    sum_fe, sum_wfe, sum_qee = fold(fe), fold(w * fe), fold(qw_row * e * e)
     arrived(s["exr"], "ex")
     ex = s["ex"][...]
     for k in range(n_cell - 1):
@@ -377,26 +398,18 @@
     t1q = jnp.concatenate([ex[nq + i : nq + i + 1] for i in range(nq)], axis=1)
     bb, bwb, wbwb, wbwwb, t00, t01, t02, t11 = [ex[2 * nq + i : 2 * nq + i + 1] for i in range(8)]
     zq = t0q * qw_row
-    zq8 = jnp.broadcast_to(zq, (8, queries))
-    t0k = dot_l(zq8, qb[...], NT)[0:1]
+    z3 = stack(zq)
+    t0k = unstack(mxu(z3, qb[...], NT), 1)
     t0k2 = jnp.concatenate([t0k[:, :128], t0k[:, 128:]], axis=0)
     gs = GROUP_SIZE
     s["az"][...] = jnp.concatenate([t0, 0.25 * t1 + 0.5 * t0k2 + (gs / 16) * t0], axis=0)
     for k in spread_order(NZ):
-        send(s["az"], s["azr"].at[z], "az", z_peer(k))
+        send(s["az"], s["azr"].at[z], "af" if k in FAR else "az", z_peer(k))
     keep(s["az"], s["azr"].at[z], "az")
 
-    arrived(s["mf"], "ma")
-    zg = gram(zq8)[0:1]
+    zg = unstack(mxu(z3, s["g_hi"][...], NN) + mxu(z3, s["g_lo"][...], NN), 1)
     q00, q01, zgz = fold(zq * t0q), fold(zq * t1q), fold(zg * zq)
     sw = t[3:4]
-    m = s["mf"][...]
-    f = m * qw_row
-    fm = f * m
-    sum_fm, sum_wfm, sum_wwfm = fold(fm), fold(w * fm), fold(w * w * fm)
-    e = gram(f)
-    fe = f * e
-    sum_fe, sum_wfe, sum_qee = fold(fe), fold(w * fe), fold(qw_row * e * e)
     mu0 = bb
     mu1 = bwb + sum_fm + 0.25 * t00
     mu2 = wbwb + 2.0 * sum_wfm + sum_fe + 0.5 * (t01 + q00) + (gs / 16) * t00
@@ -419,28 +432,28 @@
     s["uv"][...] = u
     s["w2l"][...] = w * u + dot_l((w * m + e) * qw_row, qb[...], NT)
 
-    arrived(s["azr"], "az")
-    for i in range(4):
-        s["ay"][:, i * 128 : (i + 1) * 128] = s["azr"][:, i, :]
-    for k in spread_order(NY):
-        send(s["ay"], s["ayr"].at[y], "ay", y_peer(k))
-    keep(s["ay"], s["ayr"].at[y], "ay")
+    n_far = len(FAR)
+    arrived(s["azr"].at[: NZ - n_far], "az")
+    for k in range(NZ):
+        if k not in FAR:
+            for j in spread_order(NY):
+                send(s["azr"].at[to_z(k)], s["ayr"].at[y, to_z(k)], "ay", y_peer(j))
+    arrived(s["azr"].at[:n_far], "af")
+    for k in FAR:
+        for j in spread_order(NY):
+            send(s["azr"].at[to_z(k)], s["ayr"].at[y, to_z(k)], "ay", y_peer(j))
+    keep(s["azr"], s["ayr"].at[y], "ay")
     arrived(s["mzr"], "mz")
     s["my"][...] = jnp.sum(s["mzr"][...], axis=0)
     for k in spread_order(NY):
         send(s["my"], s["myr"].at[y], "my", y_peer(k))
     keep(s["my"], s["myr"].at[y], "my")
     arrived(s["ayr"], "ay")
-    spread = dot_r(pick, s["ayr"][...].reshape(groups, 512), NN)
+    gathered = jnp.concatenate([s["ayr"][:, :, i, :].reshape(groups, 128) for i in range(4)], axis=1)
+    spread = dot_r(pick, gathered, NN)
     t0b = spread[:, :cells]
     s["w1v"][...] = s["uv"][...] + 0.25 * t0b
     s["w2v"][...] = s["w2l"][...] + (0.25 * (w * t0b) + spread[:, cells:])
-    outs += [
-        pltpu.make_async_copy(s["w1v"], w1_out, s["out"].at[1]),
-        pltpu.make_async_copy(s["w2v"], w2_out, s["out"].at[2]),
-    ]
-    outs[1].start()
-    outs[2].start()
     arrived(s["myr"], "my")
     mu = jnp.sum(jnp.sum(s["myr"][...], axis=0), axis=1, keepdims=True)
     mu0, mu1, mu2, mu3 = [mu[i : i + 1] for i in range(4)]
@@ -450,9 +463,14 @@
     alpha1 = rr1 / (up * up * mu1 - 2.0 * alpha0 * up * mu2 + alpha0 * alpha0 * mu3)
     c1 = alpha0 + alpha1 * up
     c2 = alpha0 * alpha1
-    s["cv"][...] = jnp.concatenate([jnp.broadcast_to(c, (4, cells)) for c in (c1, c2)], axis=0)
-    outs.append(pltpu.make_async_copy(s["cv"], c_out, s["out"].at[3]))
-    outs[3].start()
+    outs = []
+    for i in range(4):
+        part = slice(i * blk // 4, (i + 1) * blk // 4)
+        s["xv"][part] = c1 * s["bv"][part] - c2 * s["w1v"][part]
+        s["rv"][part] = s["bv"][part] - c1 * s["w1v"][part] + c2 * s["w2v"][part]
+        for j, (src, dst) in enumerate(((s["xv"], x_out), (s["rv"], r_out))):
+            outs.append(pltpu.make_async_copy(src.at[part], dst.at[part], s["out"].at[i, j]))
+            outs[-1].start()
 
     for name, ref in (
         ("z", s["ar"].at[: NZ - 1]),
@@ -469,7 +487,8 @@
         ("gd", s["gc"]),
         ("gr", s["gr"]),
         ("ga", s["gr"]),
-        ("az", s["azr"].at[: NZ - 1]),
+        ("az", s["azr"].at[: NZ - 1 - n_far]),
+        ("af", s["azr"].at[:n_far]),
         ("ay", s["ayr"].at[: NY - 1]),
         ("mz", s["mzr"].at[: NZ - 1]),
         ("my", s["myr"].at[: NY - 1]),
@@ -479,36 +498,21 @@
         copy.wait()
 
 
-def combine(b_in, w1_in, w2_in, c_in, x_out, r_out, b, w1, w2, c, x, r, load, load_c, store):
-    blk = b.shape[0]
-    steps = store.shape[0]
-    n = blk // steps
-    get_c = pltpu.make_async_copy(c_in, c, load_c)
-    get_c.start()
-    gets, puts = [], []
+def hand_on(x_in, r_in, x_out, r_out, x, r, load, store):
+    steps = load.shape[0]
+    n = x.shape[0] // steps
+    moves = []
     for i in range(steps):
         part = pl.ds(i * n, n)
-        gets.append(
-            [
-                pltpu.make_async_copy(src.at[part], dst.at[part], load.at[i, j])
-                for j, (src, dst) in enumerate(((b_in, b), (w1_in, w1), (w2_in, w2)))
-            ]
-        )
-        for copy in gets[-1]:
-            copy.start()
-    get_c.wait()
-    c1, c2 = c[0:1], c[4:5]
-    for i in range(steps):
-        part = pl.ds(i * n, n)
-        for copy in gets[i]:
-            copy.wait()
-        x[part] = c1 * b[part] - c2 * w1[part]
-        r[part] = b[part] - c1 * w1[part] + c2 * w2[part]
-        for j, (src, dst) in enumerate(((x, x_out), (r, r_out))):
-            puts.append(pltpu.make_async_copy(src.at[part], dst.at[part], store.at[i, j]))
-            puts[-1].start()
-    for copy in puts:
-        copy.wait()
+        for j, (src, via, dst) in enumerate(((x_in, x, x_out), (r_in, r, r_out))):
+            get = pltpu.make_async_copy(src.at[part], via.at[part], load.at[i, j])
+            get.start()
+            moves.append((get, pltpu.make_async_copy(via.at[part], dst.at[part], store.at[i, j])))
+    for get, put in moves:
+        get.wait()
+        put.start()
+    for get, put in moves:
+        put.wait()
 
 
 def local(detail_rows, row_block, block_weight, block_group, query_matrix, query_weight, query_noisy, group_noisy):
@@ -517,9 +521,9 @@
     out = jax.ShapeDtypeStruct((blk, cells), F32)
     taken = pl.pallas_call(
         functools.partial(kernel, tuple(scratch)),
-        out_shape=(out, out, out, jax.ShapeDtypeStruct((8, cells), F32)),
+        out_shape=(out, out),
         in_specs=[pl.BlockSpec(memory_space=pl.ANY)] * 8,
-        out_specs=(pl.BlockSpec(memory_space=pl.ANY),) * 4,
+        out_specs=(pl.BlockSpec(memory_space=pl.ANY),) * 2,
         scratch_shapes=list(scratch.values()),
         compiler_params=pltpu.CompilerParams(
             collective_id=0, has_side_effects=True, vmem_limit_bytes=60 * 1024 * 1024
@@ -535,14 +539,11 @@
         group_noisy,
     )
     return pl.pallas_call(
-        combine,
+        hand_on,
         out_shape=(out, out),
-        in_specs=[pl.BlockSpec(memory_space=pl.ANY)] * 4,
+        in_specs=[pl.BlockSpec(memory_space=pl.ANY)] * 2,
         out_specs=(pl.BlockSpec(memory_space=pl.ANY),) * 2,
-        scratch_shapes=[pltpu.VMEM((blk, cells), F32)] * 3
-        + [pltpu.VMEM((8, cells), F32)]
-        + [pltpu.VMEM((blk, cells), F32)] * 2
-        + [pltpu.SemaphoreType.DMA((4, 3)), pltpu.SemaphoreType.DMA, pltpu.SemaphoreType.DMA((4, 2))],
+        scratch_shapes=[pltpu.VMEM((blk, cells), F32)] * 2 + [pltpu.SemaphoreType.DMA((2, 2))] * 2,
         compiler_params=pltpu.CompilerParams(vmem_limit_bytes=60 * 1024 * 1024),
     )(*taken)
 

time: 57.4 us -> 55.9 us (0.974)
  Pallas kernels: 56.5 us -> 55 us
    pallas_call x1, Pallas kernels: 54.7 us -> 53.4 us  [local(): pl.pallas_call(functools.partial(kernel, tuple(scratch)), out_shape=(out,...]
where the time goes in v3:
time: 55.9 us; the launch traced here: 55.7 us
  Pallas kernels  55 us (98%)
  between operations  0.64 us (1%)
    pallas_call x1, Pallas kernels, local(): pl.pallas_call(functools.partial(kernel, tuple(scratch)), out_shape=(out,...  53.4 us
    pallas_call x1, Pallas kernels, local(): pl.pallas_call(hand_on, out_shape=(out, out), in_specs=[pl.BlockSpec(memo...  1.63 us

profile of v3, /device:TPU:1, one launch (start us, length us, event | category | flops | bytes accessed | tf_op | source)
XLA Modules:
  0.0 55.7 jit_solution(7992697125225382620)
XLA Ops:
  0.6 53.4 %shard_map.95 = (f32[128,256]{1,0:T(8,128)}, f32[128,256]{1,0:T(8,128)}) custom-call(f32[128,256]{1,0:T(8,128)} %dr.1, s32[1,128]{1,0:T(1,128)} %bitcast.5, s32[1,128]{1,0:T(1,128)} %bitcast.6, s32[1,128]{1,0:T(1,128)} %bitcast.7, s32[256,512]{1,0:T(8,128)} %qm.1, f32[1,512]{1,0:T(1,128)} %bitcast.4, f32[128,512]{1,0:T(8,128)} %qn.1, f32[64,256]{1,0:T(8,128)} %gn.1), custom_call_target="tpu_custom_call" | custom-call | tf_op jit(solution)/shard_map/pallas_call | solution.py:522
  54.1 1.6 %shard_map.96 = (f32[128,256]{1,0:T(8,128)}, f32[128,256]{1,0:T(8,128)}) custom-call(f32[128,256]{1,0:T(8,128)} %get-tuple-element.4.x_in, f32[128,256]{1,0:T(8,128)} %get-tuple-element.5.r_in), custom_call_target="tpu_custom_call" | custom-call | tf_op jit(solution)/shard_map/pallas_call | solution.py:541

commit v4 on v3

--- a/solution.py
+++ b/solution.py
@@ -70,7 +70,7 @@
     zr = blk // NZ
     shapes = {
         "qi": ((cells, queries), jnp.int32),
-        "drv": ((blk, cells), F32),
+        "drv": ((NZ, zr, cells), F32),
         "rbv": ((1, blk), jnp.int32),
         "qb": ((cells, queries), BF16),
         "bwv": ((1, blk), jnp.int32),
@@ -79,13 +79,18 @@
         "qnv": ((blk, queries), F32),
         "gnv": ((groups, cells), F32),
         "ar": ((NZ, zr, cells), F32),
-        "ai": ((NZ, 1, blk), jnp.int32),
+        "ai": ((NZ, NY, 1, blk), jnp.int32),
+        "zs": ((NZ, zr, cells), F32),
         "sy": ((NY, zr // NY, NZ, cells), F32),
         "br": ((NY, zr // NY, NZ, cells), F32),
-        "bi": ((NY, NZ, 1, blk), jnp.int32),
+        "bi": ((NY, 1, blk), jnp.int32),
         "md": ((8, blk), F32),
         "mdr": ((NY, 8, blk), F32),
-        "gz": ((4 * groups, NY * blk), BF16),
+        "me": ((2, blk), F32),
+        "mer": ((NZ, 2, blk), F32),
+        "mx": ((8, 128), F32),
+        "mxr": ((n_cell - 1, 8, 128), F32),
+        "wv": ((blk, 128), F32),
         "tp": ((groups, 3 * cells), F32),
         "ty": ((NY - 1, NZ, 3 * cells), F32),
         "pz": ((NZ, 8, 128), F32),
@@ -130,15 +135,16 @@
     return out
 
 
-PHASES = ("z", "zi", "y", "yi", "md", "ty", "tz", "ex", "mr", "ma", "gc", "gd", "gr", "ga", "az", "af", "ay", "mz", "my")
-
-
-FAR = [k for k in range(1, NZ) if min(k, NZ - k) > 5]
+PHASES = ("me", "mx", "z", "zi", "y", "yi", "md", "ty", "tz", "ex", "mr", "ma", "gc", "gd", "gr", "ga", "az", "af", "ay", "mz", "my")
+
+
+def far_along_z():
+    return [k for k in range(1, NZ) if min(k, NZ - k) > 5 * NZ // 16]
 
 
 def kernel(names, dr, rb, bw, bg, qm, qw, qn, gn, x_out, r_out, *refs):
     s = dict(zip(names, refs))
-    blk, cells = dr.shape
+    blk, cells = rb.shape[1], dr.shape[2]
     queries = qm.shape[1]
     groups = gn.shape[0]
     n_cell = NX * NC
@@ -152,6 +158,7 @@
     z, y = geo // NY, lax.rem(geo, NY)
     x, core = cell // NC, lax.rem(cell, NC)
     mate = 1 - core
+    far = far_along_z()
 
     def to_z(k):
         return lax.rem(z + k, NZ)
@@ -215,9 +222,6 @@
     ]
     for copy in loads:
         copy.start()
-    keep(dr.at[rows(z, zr)], s["ar"].at[z], "z")
-    keep(rb, s["ai"].at[z], "zi")
-
     loads[2].wait()
     qb = s["qb"]
     qb[...] = s["qi"][...].astype(F32).astype(BF16)
@@ -232,14 +236,23 @@
     loads[4].wait()
     w_row = s["bwv"][...].astype(F32)
     bg_row = s["bgv"][...].astype(F32)
+    s["me"][...] = jnp.concatenate([w_row, bg_row], axis=0)
     s["md"][...] = jnp.concatenate([w_row, bg_row] + [jnp.zeros_like(w_row)] * 6, axis=0)
     loads[0].wait()
     loads[1].wait()
+    for yy in range(NY):
+        for kk in range(sr):
+            s["sy"][yy, kk] = s["drv"][:, yy * sr + kk, :]
     pl.semaphore_wait(barrier, len(greet))
 
+    for k in spread_order(NY):
+        send(s["sy"].at[to_y(k)], s["br"].at[y], "y", y_peer(k))
+        send(s["rbv"], s["bi"].at[y], "yi", y_peer(k))
     for k in spread_order(NZ):
-        send(s["drv"].at[rows(to_z(k), zr)], s["ar"].at[z], "z", z_peer(k))
-        send(s["rbv"], s["ai"].at[z], "zi", z_peer(k))
+        send(s["me"], s["mer"].at[z], "me", z_peer(k))
+    keep(s["sy"].at[y], s["br"].at[y], "y")
+    keep(s["rbv"], s["bi"].at[y], "yi")
+    keep(s["me"], s["mer"].at[z], "me")
     for k in spread_order(NY):
         send(s["md"], s["mdr"].at[y], "md", y_peer(k))
     keep(s["md"], s["mdr"].at[y], "md")
@@ -249,6 +262,7 @@
         copy.wait()
     eye = lax.broadcasted_iota(jnp.int32, (blk, blk), 0) == lax.broadcasted_iota(jnp.int32, (blk, blk), 1)
     w = jnp.sum(jnp.where(eye, w_row, 0.0), axis=1, keepdims=True)
+    s["wv"][...] = jnp.broadcast_to(w, (blk, 128))
     bg_col = jnp.sum(jnp.where(eye, bg_row, 0.0), axis=1, keepdims=True)
     pick = (bg_col == lax.broadcasted_iota(jnp.int32, (blk, groups), 1).astype(F32)).astype(F32).astype(BF16)
     gather = (bg_row == lax.broadcasted_iota(jnp.int32, (groups, blk), 0).astype(F32)).astype(F32).astype(BF16)
@@ -262,37 +276,51 @@
     for k in spread_order(NX):
         send(s["gh"].at[rows(to_x(k), hx)], s["gr"].at[k - 1], "gr", x_peer(k))
 
+    arrived(s["br"], "y")
+    arrived(s["bi"], "yi")
+    for yy in range(NY):
+        for kk in range(sr):
+            s["zs"][:, yy * sr + kk, :] = s["br"][yy, kk]
+    for k in spread_order(NZ):
+        send(s["zs"].at[to_z(k)], s["ar"].at[z], "z", z_peer(k))
+        send(s["bi"], s["ai"].at[z], "zi", z_peer(k))
+    keep(s["zs"].at[z], s["ar"].at[z], "z")
+    keep(s["bi"], s["ai"].at[z], "zi")
+
     arrived(s["mdr"], "md")
     w_all = jnp.concatenate([s["mdr"][i, 0:1] for i in range(NY)], axis=1)
     bg_all = jnp.concatenate([s["mdr"][i, 1:2] for i in range(NY)], axis=1)
-    is_in = bg_all == lax.broadcasted_iota(jnp.int32, (groups, NY * blk), 0).astype(F32)
-    cube = parts(w_all * w_all * w_all, 2)
-    for i, v in enumerate([w_all, w_all * w_all, cube[0].astype(F32), cube[1].astype(F32)]):
-        s["gz"][i * groups : (i + 1) * groups] = jnp.where(is_in, v, 0.0).astype(BF16)
     mine = bg_all == (lax.broadcasted_iota(jnp.int32, (NZ, NY * blk), 0) + y * NZ).astype(F32)
     s["pz"][:, 3, :] = jnp.broadcast_to(jnp.sum(jnp.where(mine, w_all, 0.0), axis=1, keepdims=True), (NZ, 128))
     s["pz"][:, 7, :] = jnp.zeros((NZ, 128), F32)
 
-    arrived(s["ar"], "z")
-    arrived(s["ai"], "zi")
-    for yy in range(NY):
-        for kk in range(sr):
-            s["sy"][yy, kk] = s["ar"][:, yy * sr + kk, :]
-    for k in spread_order(NY):
-        send(s["sy"].at[to_y(k)], s["br"].at[y], "y", y_peer(k))
-        send(s["ai"], s["bi"].at[y], "yi", y_peer(k))
-    keep(s["sy"].at[y], s["br"].at[y], "y")
-    keep(s["ai"], s["bi"].at[y], "yi")
-
-    ids = s["ai"][...].reshape(NZ, blk).astype(F32)
-    lane = lax.broadcasted_iota(jnp.int32, (NZ, blk), 1)
+    by_z = lax.broadcasted_iota(jnp.int32, (NZ, blk), 0) * zr + y * sr
+    lane_z = lax.broadcasted_iota(jnp.int32, (NZ, blk), 1)
     id_col = jnp.concatenate(
-        [jnp.sum(jnp.where(lane == z * zr + j, ids, 0.0), axis=1, keepdims=True) for j in range(zr)], axis=0
-    )
-    spot = lax.broadcasted_iota(jnp.int32, (blk, NY * blk), 1) + z * (NY * blk)
+        [
+            jnp.sum(jnp.where(lane_z == by_z + kk, s["bi"][yy].astype(F32), 0.0), axis=1, keepdims=True)
+            for yy in range(NY)
+            for kk in range(sr)
+        ],
+        axis=0,
+    )
+    block_z = lax.rem(lax.broadcasted_iota(jnp.int32, (blk, blk), 0), NZ)
+    spot = lax.broadcasted_iota(jnp.int32, (blk, blk), 1) + (block_z * NY + y) * blk
     is_at = id_col == spot.astype(F32)
-    of_row = mxu(s["gz"][...], is_at.astype(F32).astype(BF16), NT).astype(BF16)
-    sums = dot_r(of_row, s["sy"][...].reshape(blk, cells), NN)
+    arrived(s["mer"], "me")
+    w_r, g_r = [
+        jnp.sum(jnp.where(is_at, jnp.concatenate([s["mer"][:, i, :]] * zr, axis=0), 0.0), axis=1, keepdims=True)
+        for i in range(2)
+    ]
+    c_hi, c_lo = [p.astype(F32) for p in parts(w_r * w_r * w_r, 2)]
+    column = lax.broadcasted_iota(jnp.int32, (blk, 4 * groups), 1)
+    power = jnp.where(
+        column < 2 * groups,
+        jnp.where(column < groups, w_r, w_r * w_r),
+        jnp.where(column < 3 * groups, c_hi, c_lo),
+    )
+    of_row = jnp.where(g_r == lax.rem(column, groups).astype(F32), power, 0.0).astype(BF16)
+    sums = dot_r(of_row, s["br"][...].reshape(blk, cells), TN)
     s["tp"][:, :cells] += sums[:groups]
     s["tp"][:, cells : 2 * cells] += sums[groups : 2 * groups]
     s["tp"][:, 2 * cells :] += sums[2 * groups : 3 * groups] + sums[3 * groups :]
@@ -309,26 +337,6 @@
         send(s["gs"], s["gf"].at[spot_g], "ga", x_peer(k))
     keep(s["gs"], s["gf"].at[spot_g], "ga")
 
-    arrived(s["br"], "y")
-    arrived(s["bi"], "yi")
-    ids = s["bi"][...].reshape(NY * NZ, blk).astype(F32)
-    lane = lax.broadcasted_iota(jnp.int32, (NY * NZ, blk), 1)
-    id_col = jnp.concatenate(
-        [
-            jnp.sum(jnp.where(lane == geo * sr + kk, ids, 0.0), axis=1, keepdims=True)
-            for kk in range(sr)
-        ],
-        axis=0,
-    )
-    moved = jnp.concatenate([s["br"][:, kk].reshape(NY * NZ, cells) for kk in range(sr)], axis=0)
-    here = lax.broadcasted_iota(jnp.int32, (blk, blk), 1) + geo * blk
-    place = (id_col == here.astype(F32)).astype(F32).astype(BF16)
-    b = w * dot_r(place, moved, TN) + s["base"][...]
-    s["bv"][...] = b
-    s["mp"][...] = dot_l(b, qb[...], NN)
-    for k in range(1, n_cell):
-        send(s["mp"].at[rows(to_c(k), share)], s["mr"].at[k - 1], "mr", c_peer(k))
-
     arrived(s["ty"], "ty")
     t = s["tp"][rows(y, NZ)]
     for k in range(NY - 1):
@@ -338,21 +346,36 @@
     for k in spread_order(NZ):
         send(s["pz"].at[to_z(k)], s["tz"].at[k - 1], "tz", z_peer(k))
 
-    wb = w * b
-    scal_b = [fold(b * b), fold(b * wb), fold(wb * wb), fold(wb * (w * wb))]
-
-    arrived(s["mr"], "mr")
-    m_own = s["mp"][rows(cell, share)]
-    for k in range(n_cell - 1):
-        m_own = m_own + s["mr"][k]
-    s["ms"][...] = m_own
+    arrived(s["ar"], "z")
+    arrived(s["ai"], "zi")
+    lane_z = lax.broadcasted_iota(jnp.int32, (NZ, blk), 1)
+    id_col = jnp.concatenate(
+        [
+            jnp.sum(
+                jnp.where(lane_z == geo * sr + kk, s["ai"][:, yy].reshape(NZ, blk).astype(F32), 0.0),
+                axis=1,
+                keepdims=True,
+            )
+            for yy in range(NY)
+            for kk in range(sr)
+        ],
+        axis=0,
+    )
+    moved = jnp.concatenate([s["ar"][:, j, :] for j in range(zr)], axis=0)
+    here = lax.broadcasted_iota(jnp.int32, (blk, blk), 1) + geo * blk
+    place = (id_col == here.astype(F32)).astype(F32).astype(BF16)
+    b = w * dot_r(place, moved, TN) + s["base"][...]
+    s["bv"][...] = b
+    s["mp"][...] = dot_l(b, qb[...], NN)
     for k in range(1, n_cell):
-        send(s["ms"], s["mf"].at[rows(cell, share)], "ma", c_peer(k))
-    keep(s["ms"], s["mf"].at[rows(cell, share)], "ma")
+        send(s["mp"].at[rows(to_c(k), share)], s["mr"].at[k - 1], "mr", c_peer(k))
 
     held = s["gf"].at[rows(core, half)]
     arrived(held, "ga")
     send(held, held, "gd", mate_peer)
+
+    wb = w * b
+    scal_b = [fold(b * b), fold(b * wb), fold(wb * wb), fold(wb * (w * wb))]
 
     arrived(s["tz"], "tz")
     t = s["pz"][z]
@@ -381,14 +404,25 @@
         hi, lo = s["g_hi"][...], s["g_lo"][...]
         return mxu(p[0], hi, NN) + mxu(p[0], lo, NN) + mxu(p[1], hi, NN) + mxu(p[1], lo, NN) + mxu(p[2], hi, NN)
 
-    arrived(s["mf"], "ma")
-    m = s["mf"][...]
-    f = m * qw_row
-    fm = f * m
-    sum_fm, sum_wfm, sum_wwfm = fold(fm), fold(w * fm), fold(w * w * fm)
-    e = gram(f)
+    arrived(s["mr"], "mr")
+    m_own = s["mp"][rows(cell, share)]
+    for k in range(n_cell - 1):
+        m_own = m_own + s["mr"][k]
+    s["ms"][...] = m_own
+    w_own = s["wv"][rows(cell, share)][:, :1]
+    f = m_own * qw_row
+    fm = f * m_own
+    f3 = stack(f)
+    e = unstack(mxu(f3, s["g_hi"][...], NN) + mxu(f3, s["g_lo"][...], NN), share)
     fe = f * e
-    sum_fe, sum_wfe, sum_qee = fold(fe), fold(w * fe), fold(qw_row * e * e)
+    s["mx"][...] = jnp.concatenate(
+        [fold(v) for v in (fm, w_own * fm, w_own * w_own * fm, fe, w_own * fe, qw_row * e * e)]
+        + [jnp.zeros((2, 128), F32)],
+        axis=0,
+    )
+    for k in range(1, n_cell):
+        send(s["mx"], s["mxr"].at[k - 1], "mx", c_peer(k))
+
     arrived(s["exr"], "ex")
     ex = s["ex"][...]
     for k in range(n_cell - 1):
@@ -404,12 +438,20 @@
     gs = GROUP_SIZE
     s["az"][...] = jnp.concatenate([t0, 0.25 * t1 + 0.5 * t0k2 + (gs / 16) * t0], axis=0)
     for k in spread_order(NZ):
-        send(s["az"], s["azr"].at[z], "af" if k in FAR else "az", z_peer(k))
+        send(s["az"], s["azr"].at[z], "af" if k in far else "az", z_peer(k))
     keep(s["az"], s["azr"].at[z], "az")
+    for k in range(1, n_cell):
+        send(s["ms"], s["mf"].at[rows(cell, share)], "ma", c_peer(k))
+    keep(s["ms"], s["mf"].at[rows(cell, share)], "ma")
 
     zg = unstack(mxu(z3, s["g_hi"][...], NN) + mxu(z3, s["g_lo"][...], NN), 1)
     q00, q01, zgz = fold(zq * t0q), fold(zq * t1q), fold(zg * zq)
     sw = t[3:4]
+    arrived(s["mxr"], "mx")
+    mx = s["mx"][...]
+    for k in range(n_cell - 1):
+        mx = mx + s["mxr"][k]
+    sum_fm, sum_wfm, sum_wwfm, sum_fe, sum_wfe, sum_qee = [mx[i : i + 1] for i in range(6)]
     mu0 = bb
     mu1 = bwb + sum_fm + 0.25 * t00
     mu2 = wbwb + 2.0 * sum_wfm + sum_fe + 0.5 * (t01 + q00) + (gs / 16) * t00
@@ -428,18 +470,14 @@
     for k in spread_order(NZ):
         send(s["mz"], s["mzr"].at[z], "mz", z_peer(k))
     keep(s["mz"], s["mzr"].at[z], "mz")
-    u = w * s["bv"][...] + dot_l(f, qb[...], NT)
-    s["uv"][...] = u
-    s["w2l"][...] = w * u + dot_l((w * m + e) * qw_row, qb[...], NT)
-
-    n_far = len(FAR)
+    n_far = len(far)
     arrived(s["azr"].at[: NZ - n_far], "az")
     for k in range(NZ):
-        if k not in FAR:
+        if k not in far:
             for j in spread_order(NY):
                 send(s["azr"].at[to_z(k)], s["ayr"].at[y, to_z(k)], "ay", y_peer(j))
     arrived(s["azr"].at[:n_far], "af")
-    for k in FAR:
+    for k in far:
         for j in spread_order(NY):
             send(s["azr"].at[to_z(k)], s["ayr"].at[y, to_z(k)], "ay", y_peer(j))
     keep(s["azr"], s["ayr"].at[y], "ay")
@@ -448,6 +486,14 @@
     for k in spread_order(NY):
         send(s["my"], s["myr"].at[y], "my", y_peer(k))
     keep(s["my"], s["myr"].at[y], "my")
+    arrived(s["mf"], "ma")
+    m = s["mf"][...]
+    f = m * qw_row
+    e = gram(f)
+    u = w * s["bv"][...] + dot_l(f, qb[...], NT)
+    s["uv"][...] = u
+    s["w2l"][...] = w * u + dot_l((w * m + e) * qw_row, qb[...], NT)
+
     arrived(s["ayr"], "ay")
     gathered = jnp.concatenate([s["ayr"][:, :, i, :].reshape(groups, 128) for i in range(4)], axis=1)
     spread = dot_r(pick, gathered, NN)
@@ -473,6 +519,8 @@
             outs[-1].start()
 
     for name, ref in (
+        ("me", s["mer"].at[: NZ - 1]),
+        ("mx", s["mxr"]),
         ("z", s["ar"].at[: NZ - 1]),
         ("zi", s["ai"].at[: NZ - 1]),
         ("y", s["br"].at[: NY - 1]),
@@ -529,7 +577,7 @@
             collective_id=0, has_side_effects=True, vmem_limit_bytes=60 * 1024 * 1024
         ),
     )(
-        detail_rows,
+        detail_rows.reshape(NZ, -1, cells),
         row_block.reshape(1, -1),
         block_weight.reshape(1, -1),
         block_group.reshape(1, -1),

time: 55.9 us -> 52.5 us (0.939)
  Pallas kernels: 55 us -> 51.5 us
    pallas_call x1, Pallas kernels: 53.4 us -> 49.8 us  [local(): pl.pallas_call(functools.partial(kernel, tuple(scratch)), out_shape=(out,...]
where the time goes in v4:
time: 52.5 us; the launch traced here: 52.1 us
  Pallas kernels  51.5 us (98%)
  between operations  0.64 us (1%)
    pallas_call x1, Pallas kernels, local(): pl.pallas_call(functools.partial(kernel, tuple(scratch)), out_shape=(out,...  49.8 us
    pallas_call x1, Pallas kernels, local(): pl.pallas_call(hand_on, out_shape=(out, out), in_specs=[pl.BlockSpec(memo...  1.63 us

profile of v4, /device:TPU:1, one launch (start us, length us, event | category | flops | bytes accessed | tf_op | source)
XLA Modules:
  0.0 52.1 jit_solution(2433836639562792704)
XLA Ops:
  0.6 49.8 %shard_map.95 = (f32[128,256]{1,0:T(8,128)}, f32[128,256]{1,0:T(8,128)}) custom-call(f32[16,8,256]{2,1,0:T(8,128)} %bitcast.5, s32[1,128]{1,0:T(1,128)} %bitcast.7, s32[1,128]{1,0:T(1,128)} %bitcast.8, s32[1,128]{1,0:T(1,128)} %bitcast.9, s32[256,512]{1,0:T(8,128)} %qm.1, f32[1,512]{1,0:T(1,128)} %bitcast.6, f32[128,512]{1,0:T(8,128)} %qn.1, f32[64,256]{1,0:T(8,128)} %gn.1), custom_call_target="tpu_custom_call" | custom-call | tf_op jit(solution)/shard_map/pallas_call | solution.py:570
  50.5 1.6 %shard_map.96 = (f32[128,256]{1,0:T(8,128)}, f32[128,256]{1,0:T(8,128)}) custom-call(f32[128,256]{1,0:T(8,128)} %get-tuple-element.4.x_in, f32[128,256]{1,0:T(8,128)} %get-tuple-element.5.r_in), custom_call_target="tpu_custom_call" | custom-call | tf_op jit(solution)/shard_map/pallas_call | solution.py:589
